TPU v7x, 128 devices: a whole 4x4x4 slice. The times are simulated.
128 devices in a mesh: lat: 16 (over y_lo, z, core), lon: 8 (over x, y_hi).
Axes of the slice: x: 4, y: 4 (y_hi: 2, y_lo: 2; y = y_hi * 2 + y_lo), z: 4, core: 2. Of those that a mesh axis runs over, the one named last changes fastest.
Arguments:
- tokens: bfloat16 [2, 192, 384, 512], P(None, 'lat', 'lon'), may hold values from -6 to 6
- region: int32 [192, 384], P('lat', 'lon'), may hold values from 0 to 3
- w_qkv: bfloat16 [512, 1536], replicated, may hold values from -0.25 to 0.25
- w_proj: bfloat16 [512, 512], replicated, may hold values from -0.25 to 0.25
- w_merge: bfloat16 [2048, 1024], replicated, may hold values from -0.125 to 0.125
- d_merged: bfloat16 [2, 96, 192, 1024], P(None, 'lat', None, 'lon'), may hold values from -6 to 6
Outputs:
- merged: bfloat16 [2, 96, 192, 1024], P(None, 'lat', None, 'lon')
- grad_x: float32 [2, 192, 384, 512], P(None, 'lat', 'lon')
- grad_qkv: float32 [512, 1536], replicated
- grad_proj: float32 [512, 512], replicated
All inputs are finite; a program needn't handle non-finite values.
Results may differ from a plain program's by a relative error of at most 0.015.
Values may be sent and summed in bfloat16 or wider, within the bound.
A program may use at most 128 MiB of HBM per device.

v0:
```python
import jax
import jax.numpy as jnp
from jax import lax
from jax.sharding import PartitionSpec as P

D = 512
D2 = 1024
HEADS = 8
LEV = 2
WIN_LAT = 6
WIN_LON = 12


EPS = 1e-05


def from_behind(x, axis, by):
    size = lax.axis_size(axis)
    return lax.ppermute(x, axis, [(i, (i + by) % size) for i in range(size)])


def for_sending(x):

    def short(part):
        return part.astype(jnp.bfloat16) if part.dtype == jnp.float32 else part

    return jax.tree.map(short, x)


def layer_norm(value):
    average = jnp.mean(value, -1, keepdims=True)
    centred = value - average
    variance = jnp.mean(centred * centred, -1, keepdims=True)
    return centred * lax.rsqrt(variance + EPS)


def norm_back(value, grad):
    average = jnp.mean(value, -1, keepdims=True)
    centred = value - average
    variance = jnp.mean(centred * centred, -1, keepdims=True)
    inverse = lax.rsqrt(variance + EPS)
    standard = centred * inverse
    return inverse * (
        grad
        - jnp.mean(grad, -1, keepdims=True)
        - standard * jnp.mean(grad * standard, -1, keepdims=True)
    )


def to_windows(field):
    levels, lat_rows, lon_cols, feature = field.shape
    field = field.reshape(
        levels, lat_rows // WIN_LAT, WIN_LAT, lon_cols // WIN_LON, WIN_LON, feature
    )
    field = field.transpose(1, 3, 0, 2, 4, 5)
    return field.reshape(-1, levels * WIN_LAT * WIN_LON, feature)


def from_windows(field, lat_rows, lon_cols):
    feature = field.shape[-1]
    field = field.reshape(lat_rows // WIN_LAT, lon_cols // WIN_LON, LEV, WIN_LAT, WIN_LON, feature)
    field = field.transpose(2, 0, 3, 1, 4, 5)
    return field.reshape(LEV, lat_rows, lon_cols, feature)


def split_qkv(qkv):
    win_count, length, _ = qkv.shape
    split_heads = qkv.reshape(win_count, length, 3, HEADS, D // HEADS)
    return (split_heads[:, :, 0], split_heads[:, :, 1], split_heads[:, :, 2])


def attend(qkv, allowed):
    win_count, length, _ = qkv.shape
    queries, keys_h, values = split_qkv(qkv)
    score_scale = (D // HEADS) ** (-0.5)
    scores = (
        jnp.einsum("wqhd,wkhd->whqk", queries, keys_h, preferred_element_type=jnp.float32)
        * score_scale
    )
    weights = jnp.where(allowed[:, None], jnp.exp(scores), 0.0)
    soft_weights = weights / jnp.sum(weights, -1, keepdims=True)
    soft_bf = soft_weights.astype(jnp.bfloat16)
    mixed_out = jnp.einsum("whqk,wkhd->wqhd", soft_bf, values, preferred_element_type=jnp.float32)
    return (mixed_out.astype(jnp.bfloat16).reshape(win_count, length, D), soft_weights, soft_bf)


def attend_back(qkv, soft_weights, soft_bf, d_mixed):
    win_count, length, _ = qkv.shape
    queries, keys_h, values = split_qkv(qkv)
    score_scale = (D // HEADS) ** (-0.5)
    grad_heads = d_mixed.reshape(win_count, length, HEADS, D // HEADS)
    d_soft = jnp.einsum("wqhd,wkhd->whqk", grad_heads, values, preferred_element_type=jnp.float32)
    d_values = jnp.einsum(
        "whqk,wqhd->wkhd", soft_bf, grad_heads, preferred_element_type=jnp.float32
    )
    d_scores = soft_weights * (d_soft - jnp.sum(soft_weights * d_soft, -1, keepdims=True))
    d_scores_bf = d_scores.astype(jnp.bfloat16)
    d_queries = (
        jnp.einsum("whqk,wkhd->wqhd", d_scores_bf, keys_h, preferred_element_type=jnp.float32)
        * score_scale
    )
    d_keys = (
        jnp.einsum("whqk,wqhd->wkhd", d_scores_bf, queries, preferred_element_type=jnp.float32)
        * score_scale
    )
    stacked = jnp.stack([d_queries, d_keys, d_values], 2)
    return stacked.astype(jnp.bfloat16).reshape(win_count, length, 3 * D)


def per_device(tokens, region, w_qkv, w_proj, w_merge, d_merged):
    levels, lat_rows, lon_cols, feature = tokens.shape
    half_lat = WIN_LAT // 2
    half_lon = WIN_LON // 2
    lat_count = lax.axis_size("lat")
    lon_count = lax.axis_size("lon")
    region_bf = region.astype(jnp.bfloat16)
    edge_x, edge_r = from_behind((tokens[:, :, :half_lon], region_bf[:, :half_lon]), "lon", -1)
    shifted_x = jnp.concatenate([tokens[:, :, half_lon:], edge_x], 2)
    shifted_r = jnp.concatenate([region_bf[:, half_lon:], edge_r], 1)
    below_x, below_r = from_behind((shifted_x[:, :half_lat], shifted_r[:half_lat]), "lat", -1)
    rolled = jnp.concatenate([shifted_x[:, half_lat:], below_x], 1)
    region_rolled = jnp.concatenate([shifted_r[half_lat:], below_r], 0).astype(jnp.float32)
    global_rows = lax.axis_index("lat") * lat_rows + jnp.arange(lat_rows, dtype=jnp.int32)
    edge_rows = (global_rows >= lat_count * lat_rows - half_lat).astype(jnp.float32)
    window_keys = region_rolled + 4.0 * edge_rows[:, None]
    key_win = to_windows(
        jnp.broadcast_to(window_keys[None, :, :, None], (levels, lat_rows, lon_cols, 1))
    )[:, :, 0]
    allowed = key_win[:, :, None] == key_win[:, None, :]
    rolled_win = to_windows(rolled)
    win_count = rolled_win.shape[0]
    rolled_win_f = rolled_win.astype(jnp.float32)
    normed_win = layer_norm(rolled_win_f).astype(jnp.bfloat16)
    flat_norm = normed_win.reshape(-1, feature)
    qkv = jnp.dot(flat_norm, w_qkv, preferred_element_type=jnp.float32).astype(jnp.bfloat16)
    qkv_win = qkv.reshape(win_count, -1, 3 * feature)
    mixed_out, soft_weights, soft_bf = attend(qkv_win, allowed)
    mixed_flat = mixed_out.reshape(-1, feature)
    branch = jnp.dot(mixed_flat, w_proj, preferred_element_type=jnp.float32).astype(jnp.bfloat16)
    branch = from_windows(branch.reshape(win_count, -1, feature), lat_rows, lon_cols)
    top_rows = from_behind(branch[:, -half_lat:], "lat", 1)
    lifted = jnp.concatenate([top_rows, branch[:, :-half_lat]], 1)
    left_cols = from_behind(lifted[:, :, -half_lon:], "lon", 1)
    restored = jnp.concatenate([left_cols, lifted[:, :, :-half_lon]], 2)
    stream = (tokens.astype(jnp.float32) + restored.astype(jnp.float32)).astype(jnp.bfloat16)
    half_rows = lat_rows // 2
    half_cols = lon_cols // 2
    grouped = stream.reshape(levels, half_rows, 2, half_cols, 2, feature).transpose(
        0, 1, 3, 4, 2, 5
    )
    grouped_f = grouped.reshape(levels, half_rows, half_cols, 4 * feature).astype(jnp.float32)
    merge_in = layer_norm(grouped_f).astype(jnp.bfloat16)
    full_out = jnp.dot(
        merge_in.reshape(-1, 4 * feature), w_merge, preferred_element_type=jnp.float32
    )
    full_out = full_out.astype(jnp.bfloat16).reshape(levels, half_rows, half_cols, D2)
    merged = lax.all_to_all(full_out, "lon", split_axis=3, concat_axis=2, tiled=True)
    d_local = lax.all_to_all(d_merged, "lon", split_axis=2, concat_axis=3, tiled=True)
    d_in = jnp.dot(d_local.reshape(-1, D2), w_merge.T, preferred_element_type=jnp.float32)
    d_in = d_in.reshape(levels, half_rows, half_cols, 4 * feature)
    d_grouped = norm_back(grouped_f, d_in)
    d_stream = d_grouped.reshape(levels, half_rows, half_cols, 2, 2, feature).transpose(
        0, 1, 4, 2, 3, 5
    )
    d_stream = d_stream.reshape(levels, lat_rows, lon_cols, feature)
    d_branch = d_stream.astype(jnp.bfloat16)
    edge_d = from_behind(d_branch[:, :, :half_lon], "lon", -1)
    shifted_d = jnp.concatenate([d_branch[:, :, half_lon:], edge_d], 2)
    below_d = from_behind(shifted_d[:, :half_lat], "lat", -1)
    d_rolled_in = jnp.concatenate([shifted_d[:, half_lat:], below_d], 1)
    d_win = to_windows(d_rolled_in).reshape(-1, feature)
    grad_proj = jnp.dot(mixed_flat.T, d_win, preferred_element_type=jnp.float32)
    d_mixed = jnp.dot(d_win, w_proj.T, preferred_element_type=jnp.float32).astype(jnp.bfloat16)
    d_qkv = attend_back(qkv_win, soft_weights, soft_bf, d_mixed.reshape(win_count, -1, feature))
    d_flat = d_qkv.reshape(-1, 3 * feature)
    grad_qkv = jnp.dot(flat_norm.T, d_flat, preferred_element_type=jnp.float32)
    d_norm = jnp.dot(d_flat, w_qkv.T, preferred_element_type=jnp.float32).reshape(
        win_count, -1, feature
    )
    d_rolled_win = norm_back(rolled_win_f, d_norm)
    d_rolled = from_windows(d_rolled_win, lat_rows, lon_cols)
    top_d = from_behind(d_rolled[:, -half_lat:].astype(jnp.bfloat16), "lat", 1).astype(jnp.float32)
    lifted_d = jnp.concatenate([top_d, d_rolled[:, :-half_lat]], 1)
    left_d = from_behind(for_sending(lifted_d[:, :, -half_lon:]), "lon", 1)
    grad_x = d_stream + jnp.concatenate([left_d, lifted_d[:, :, :-half_lon]], 2)
    total_qkv, total_proj = lax.psum((grad_qkv, grad_proj), ("lat", "lon"))
    factor = float(levels * lat_rows * lat_count * lon_cols * lon_count) ** (-0.5)
    return (merged, grad_x, total_qkv * factor, total_proj * factor)


def solution(mesh):
    in_specs = (
        P(None, "lat", "lon", None),
        P("lat", "lon"),
        P(),
        P(),
        P(),
        P(None, "lat", None, "lon"),
    )
    out_specs = (P(None, "lat", None, "lon"), P(None, "lat", "lon", None), P(), P())
    return jax.shard_map(
        per_device, mesh=mesh, in_specs=in_specs, out_specs=out_specs, check_vma=False
    )
```

profile of v0, /device:TPU:1, one launch (start us, length us, event | category | flops | bytes accessed | tf_op | source)
XLA Modules:
  0.0 460.2 jit_solution(9779718138545998219)
XLA Ops:
  8.0 5.9 %collective-permute-start.2 = (bf16[12,6]{1,0:T(8,128)(2,1)S(1)}, bf16[12,6]{1,0:T(8,128)(2,1)S(1)}, u32[]{:S(2)}, u32[]{:S(2)}) collective-permute-start(bf16[12,6]{1,0:T(8,128)(2,1)S(1)} %bitcast.149), channel_id=1, source_target_pairs={{0,7},{1,0},{2,1},{3,2},{4,3},{5,4},{6,5},{7,6},{8,15},{9,8},{10,9... | collective-permute-start | bytes 440 | tf_op jit(solution)/shard_map/ppermute | solution.py:19
  24.9 4.9 %collective-permute-done.1 = bf16[2,3,48,512]{3,2,1,0:T(8,128)(2,1)S(1)} collective-permute-done((bf16[2,3,48,512]{3,2,1,0:T(8,128)(2,1)S(1)}, bf16[2,3,48,512]{3,2,1,0:T(8,128)(2,1)S(1)}, u32[]{:S(2)}, u32[]{:S(2)}) %collective-permute-start.1) | collective-permute-done | bytes 294944 | tf_op jit(solution)/shard_map/ppermute | solution.py:19
  46.4 5.6 %convolution_convert_fusion = bf16[1152,1536]{1,0:T(8,128)(2,1)} fusion(bf16[512,1536]{1,0:T(8,128)(2,1)S(1)} %copy-done, f32[1152,512]{1,0:T(8,128)} %reshape.223, f32[1152]{0:T(1024)S(1)} %rsqrt.31, f32[1152]{0:T(1024)S(1)} %div.43), kind=kOutput, calls=%fused_computation.6 | convolution fusion | flops 1815478272 | bytes 7480320 | tf_op jit(solution)/shard_map/dot_general | solution.py:135
  52.0 9.6 %reshape.237 = bf16[8,144,3,8,64]{4,3,2,1,0:T(8,128)(2,1)} reshape(bf16[1152,1536]{1,0:T(8,128)(2,1)} %convolution_convert_fusion) | data formatting | bytes 7077888 | tf_op jit(solution)/shard_map/reshape;reshape | solution.py:68
  61.5 6.1 %fusion.41 = (bf16[8,144,1,8,64]{4,3,2,1,0:T(8,128)(2,1)}, bf16[8,144,1,8,64]{4,3,2,1,0:T(8,128)(2,1)}, bf16[8,144,1,8,64]{4,3,2,1,0:T(8,128)(2,1)}) fusion(bf16[8,144,3,8,64]{4,3,2,1,0:T(8,128)(2,1)} %reshape.237), kind=kLoop, calls=%fused_computation.89 | loop fusion | bytes 7077888 | tf_op jit(solution)/shard_map/slice | solution.py:69
  67.7 4.4 copy.225
  72.1 4.5 copy.224
  76.6 4.5 copy.226
  81.1 5.0 %fusion.1 = (f32[8,8,144]{2,1,0:T(8,128)S(1)}, f32[8,8,144,144]{2,3,1,0:T(8,128)S(1)}) fusion(pred[8,144,144]{1,2,0:T(8,128)(4,1)S(1)} %copy-done.22, bf16[8,144,1,8,64]{1,4,3,0,2:T(8,128)(2,1)} %copy.226, bf16[8,144,1,8,64]{1,4,3,0,2:T(8,128)(2,1)} %copy.225), kind=kOutput, calls=%fused_computation.5 | convolution fusion | flops 173841408 | bytes 7870464 | tf_op jit(solution)/shard_map/wqhd,wkhd->whqk/dot_general | solution.py:77
  92.4 4.9 %reshape_reshape.18 = bf16[1152,512]{0,1:T(8,128)(2,1)} reshape(bf16[8,144,8,64]{1,0,3,2:T(8,128)(2,1)} %copy.185) | data formatting | bytes 2359296 | tf_op jit(solution)/shard_map/reshape;reshape | solution.py:138
  125.5 4.0 collective-permute-done.5
  146.5 4.2 reshape.226
  150.7 4.7 %fusion.40 = (f32[2,6,24]{2,1,0:T(8,128)S(1)}, f32[2,6,24]{2,1,0:T(8,128)S(1)}, f32[2,6,24,2048]{3,2,1,0:T(8,128)S(1)}) fusion(f32[2,6,24]{2,1,0:T(8,128)S(1)} %add_rsqrt_fusion.1, f32[2,6,24,2048]{3,2,1,0:T(8,128)} %reshape.226, f32[2,6,24]{2,1,0:T(8,128)S(1)} %broadcast_multiply_fusion.7, bf16[2,6,24,1024]{3,2,1,0:T(8,128)(2,1)S(1)} %dot_general.49, ...), kind=kOutput, calls=%fused_computation.88 | convolution fusion | flops 1210908160 | bytes 9507328 | tf_op jit(solution)/shard_map/dot_general | solution.py:159
  157.7 4.4 reshape.218
  167.9 4.3 collective-permute-done.6
  173.3 4.7 %collective-permute-start.7 = (bf16[2,3,48,512]{3,0,2,1:T(2,128)(2,1)}, bf16[2,3,48,512]{3,0,2,1:T(2,128)(2,1)}, u32[]{:S(2)}, u32[]{:S(2)}) collective-permute-start(bf16[2,3,48,512]{3,0,2,1:T(2,128)(2,1)} %pad_maximum_fusion.2), channel_id=1, source_target_pairs={{0,120},{8,0},{16,8},{24,16},{32,24},{40,32},{48,40},{56,48},{64,5... | collective-permute-start | bytes 884744 | tf_op jit(solution)/shard_map/ppermute | solution.py:19
  192.4 4.2 reshape.225
  208.8 4.6 copy.198
  213.4 8.2 %fusion.10 = bf16[8,144,1,8,64]{1,4,3,0,2:T(8,128)(2,1)} fusion(bf16[8,144,8,64]{1,3,2,0:T(8,128)(2,1)} %copy.198, f32[8,8,144,144]{2,3,1,0:T(8,128)} %copy-done.8, f32[8,8,144]{2,1,0:T(8,128)S(1)} %copy-done.29, pred[8,144,144]{1,2,0:T(8,128)(4,1)S(1)} %copy-done.23), kind=kOutput, calls=%fused_computation.35 | convolution fusion | flops 175177728 | bytes 7870464 | tf_op jit(solution)/shard_map/whqk,wqhd->wkhd/dot_general | solution.py:93
  221.6 5.5 %multiply_reduce_fusion = (f32[8,8,144]{2,1,0:T(8,128)S(1)}, f32[8,8,144,144]{2,3,1,0:T(8,128)}) fusion(f32[8,8,144]{2,1,0:T(8,128)S(1)} %copy-done.29, f32[8,8,144,144]{2,3,1,0:T(8,128)S(1)} %bitcast.135, pred[8,144,144]{1,2,0:T(8,128)(4,1)S(1)} %copy-done.23, bf16[8,144,8,64]{1,3,2,0:T(8,128)(2,1)S(1)} %copy-done.18, ...), kind=kOutput, calls=%fused_computation.2 | convolution fusion | flops 176495616 | bytes 13215744 | tf_op jit(solution)/shard_map/wqhd,wkhd->whqk/dot_general | solution.py:92
  227.1 6.2 %multiply_convert_fusion = bf16[8,8,144,144]{2,3,1,0:T(8,128)(2,1)S(1)} fusion(f32[8,8,144,144]{2,3,1,0:T(8,128)} %get-tuple-element.37, f32[8,8,144]{2,1,0:T(8,128)S(1)} %get-tuple-element.36, f32[8,8,144]{2,1,0:T(8,128)S(1)} %copy-done.29, f32[8,8,144,144]{2,3,1,0:T(8,128)S(1)} %bitcast.135, pred[8,144,144]{1,2,0:T(8,128)(4,1)S(1)} %copy-done.23), kind=kLoop, calls=%fused_computation.1 | loop fusion | flops 7962624 | bytes 13510656 | tf_op jit(solution)/shard_map/convert_element_type | solution.py:97
  240.7 7.3 %copy.211 = bf16[8,144,3,8,64]{1,0,4,3,2:T(8,128)(2,1)} copy(bf16[8,144,3,8,64]{1,4,3,0,2:T(8,128)(2,1)S(1)} %maximum_convert_fusion) | data formatting | bytes 7077888 | tf_op jit(solution)/shard_map/convert_element_type | solution.py:107
  247.9 11.0 %copy.203 = bf16[8,144,3,8,64]{4,3,2,1,0:T(8,128)(2,1)} copy(bf16[8,144,3,8,64]{1,4,3,0,2:T(8,128)(2,1)} %copy-done.3) | data formatting | bytes 7077888 | tf_op jit(solution)/shard_map/convert_element_type | solution.py:107
  259.0 10.3 %convert_element_type.179 = bf16[1152,1536]{0,1:T(8,128)(2,1)} reshape(bf16[8,144,3,8,64]{1,0,4,3,2:T(8,128)(2,1)} %copy.211) | data formatting | bytes 7077888 | tf_op jit(solution)/shard_map/convert_element_type | solution.py:107
  269.2 10.1 %convert_element_type.172 = bf16[8,144,1536]{2,1,0:T(8,128)(2,1)} reshape(bf16[8,144,3,8,64]{4,3,2,1,0:T(8,128)(2,1)} %copy.203) | data formatting | bytes 7077888 | tf_op jit(solution)/shard_map/convert_element_type | solution.py:107
  279.3 6.5 %fusion.39 = (f32[8,144]{1,0:T(8,128)S(1)}, f32[8,144]{1,0:T(8,128)S(1)}, f32[8,144,512]{2,1,0:T(8,128)}) fusion(f32[8,144]{1,0:T(8,128)S(1)} %rsqrt.34, f32[8,144,512]{2,1,0:T(8,128)} %reshape.236, f32[8,144]{1,0:T(8,128)S(1)} %div.53, bf16[8,144,1536]{2,1,0:T(8,128)(2,1)} %convert_element_type.172, bf16[512,1536]{1,0:T(8,128)(2,1)S(1)} %copy-done), kind=kOutput, calls=%fused_computation.87 | convolution fusion | flops 1814886144 | bytes 9848832 | tf_op jit(solution)/shard_map/dot_general | solution.py:177
  308.3 5.5 %copy.190 = bf16[2,6,24,1024]{2,0,1,3:T(2,128)(2,1)} copy(bf16[2,6,24,1024]{3,2,1,0:T(8,128)(2,1)S(1)} %bitcast.148) | data formatting | bytes 1179648 | tf_op jit(solution)/shard_map/reshape | solution.py:156
  313.8 6.0 %reshape.239 = bf16[8,2,18432]{2,1,0:T(2,128)(2,1)} reshape(bf16[1024,6,2,24]{3,2,1,0:T(2,128)(2,1)} %bitcast.132) | data formatting | bytes 1179648
  319.7 4.4 all-to-all-start
  333.2 6.1 %reshape.240 = bf16[1024,6,2,24]{3,2,1,0:T(2,128)(2,1)} reshape(bf16[8,2,18432]{2,1,0:T(2,128)(2,1)} %all-to-all-done) | data formatting | bytes 1179648
  339.3 8.0 %copy.191 = bf16[2,6,8,24,128]{4,3,2,1,0:T(8,128)(2,1)} copy(bf16[2,6,8,24,128]{3,0,1,4,2:T(2,128)(2,1)} %bitcast.133) | data formatting | bytes 1179648 | tf_op jit(solution)/shard_map/all_to_all | solution.py:157
  353.2 94.9 %all-reduce.3.cloned.1.call-done = (f32[512,1536]{1,0:T(8,128)}, f32[512,512]{1,0:T(8,128)}) async-done(((f32[512,1536]{1,0:T(8,128)}, f32[512,512]{1,0:T(8,128)}), (f32[512,1536]{1,0:T(8,128)}, f32[512,512]{1,0:T(8,128)})) %all-reduce.3.cloned.1.call-update) | async-done | bytes 4194320 | tf_op jit(solution)/shard_map/psum | solution.py:186
  (182 shorter events, 164.8 us)
Async XLA Ops:
  7.2 39.2 %copy-start = (bf16[512,1536]{1,0:T(8,128)(2,1)S(1)}, bf16[512,1536]{1,0:T(8,128)(2,1)}, u32[]{:S(2)}) copy-start(bf16[512,1536]{1,0:T(8,128)(2,1)} %param.8) | copy-start | bytes 4718596
  8.0 8.9 %collective-permute-start.2 = (bf16[12,6]{1,0:T(8,128)(2,1)S(1)}, bf16[12,6]{1,0:T(8,128)(2,1)S(1)}, u32[]{:S(2)}, u32[]{:S(2)}) collective-permute-start(bf16[12,6]{1,0:T(8,128)(2,1)S(1)} %bitcast.149), channel_id=1, source_target_pairs={{0,7},{1,0},{2,1},{3,2},{4,3},{5,4},{6,5},{7,6},{8,15},{9,8},{10,9... | collective-permute-start | bytes 440 | tf_op jit(solution)/shard_map/ppermute | solution.py:19
  14.9 7.0 %collective-permute-start = (bf16[2,12,6,512]{3,2,1,0:T(8,128)(2,1)S(1)}, bf16[2,12,6,512]{3,2,1,0:T(8,128)(2,1)S(1)}, u32[]{:S(2)}, u32[]{:S(2)}) collective-permute-start(bf16[2,12,6,512]{3,2,1,0:T(8,128)(2,1)S(1)} %slice.75), channel_id=1, source_target_pairs={{0,7},{1,0},{2,1},{3,2},{4,3},{5,4},{6,5},{7,6},{8,15},{9,8},{10,9... | collective-permute-start | bytes 442376 | tf_op jit(solution)/shard_map/ppermute | solution.py:19
  17.0 4.3 collective-permute-start.3
  21.9 7.9 %collective-permute-start.1 = (bf16[2,3,48,512]{3,2,1,0:T(8,128)(2,1)S(1)}, bf16[2,3,48,512]{3,2,1,0:T(8,128)(2,1)S(1)}, u32[]{:S(2)}, u32[]{:S(2)}) collective-permute-start(bf16[2,3,48,512]{3,2,1,0:T(8,128)(2,1)S(1)} %pad_maximum_fusion.3), channel_id=1, source_target_pairs={{0,120},{8,0},{16,8},{24,16},{32,24},{40,32},{48,40},{56,48},{64,5... | collective-permute-start | bytes 884744 | tf_op jit(solution)/shard_map/ppermute | solution.py:19
  36.1 5.6 %copy-start.25 = (f32[2,4,2,6,12]{4,3,2,1,0:T(8,128)}, f32[2,4,2,6,12]{4,3,2,1,0:T(8,128)S(1)}, u32[]{:S(2)}) copy-start(f32[2,4,2,6,12]{4,3,2,1,0:T(8,128)S(1)} %copy.175) | copy-start | bytes 13828
  81.1 5.0 %copy-start.16 = (bf16[8,144,1,8,64]{1,4,3,0,2:T(8,128)(2,1)S(1)}, bf16[8,144,1,8,64]{1,4,3,0,2:T(8,128)(2,1)}, u32[]{:S(2)}) copy-start(bf16[8,144,1,8,64]{1,4,3,0,2:T(8,128)(2,1)} %copy.224) | copy-start | bytes 3538948
  92.4 4.9 %copy-start.30 = (bf16[512,512]{1,0:T(8,128)(2,1)S(1)}, bf16[512,512]{1,0:T(8,128)(2,1)}, u32[]{:S(2)}) copy-start(bf16[512,512]{1,0:T(8,128)(2,1)} %param.9) | copy-start | bytes 1572868
  103.6 4.7 %copy-start.27 = (bf16[2,6,192,128]{3,2,1,0:T(8,128)(2,1)S(1)}, bf16[2,6,192,128]{3,2,1,0:T(8,128)(2,1)}, u32[]{:S(2)}) copy-start(bf16[2,6,192,128]{3,2,1,0:T(8,128)(2,1)} %param.11) | copy-start | bytes 1769476
  108.3 6.7 %collective-permute-start.4 = (bf16[2,3,48,512]{3,2,1,0:T(8,128)(2,1)}, bf16[2,3,48,512]{3,2,1,0:T(8,128)(2,1)}, u32[]{:S(2)}, u32[]{:S(2)}) collective-permute-start(bf16[2,3,48,512]{3,2,1,0:T(8,128)(2,1)} %copy.227), channel_id=1, source_target_pairs={{0,8},{8,16},{16,24},{24,32},{32,40},{40,48},{48,56},{56,64},{64,7... | collective-permute-start | bytes 884744 | tf_op jit(solution)/shard_map/ppermute | solution.py:19
  109.6 13.4 %all-to-all-start.1 = ((bf16[2,6,192,128]{3,1,0,2:T(8,128)(2,1)}), bf16[2,6,192,128]{3,1,0,2:T(8,128)(2,1)S(1)}, u32[]{:S(2)}, u32[]{:S(2)}) async-start(bf16[2,6,192,128]{3,1,0,2:T(8,128)(2,1)} %copy.192), calls=%async_computation.1 | async-start | bytes 1572864 | tf_op jit(solution)/shard_map/all_to_all | solution.py:158
  113.2 335.0 %all-reduce.3.cloned.1.call-start = ((), (), s32[]{:S(2)}) async-start(), calls=%async_computation.2 | async-start | bytes 8388608 | tf_op jit(solution)/shard_map/psum | solution.py:186
  117.4 12.2 %collective-permute-start.5 = (bf16[2,12,6,512]{3,2,1,0:T(8,128)(2,1)}, bf16[2,12,6,512]{3,2,1,0:T(8,128)(2,1)S(1)}, u32[]{:S(2)}, u32[]{:S(2)}) collective-permute-start(bf16[2,12,6,512]{3,2,1,0:T(8,128)(2,1)} %slice.108), channel_id=1, source_target_pairs={{0,1},{1,2},{2,3},{3,4},{4,5},{5,6},{6,7},{7,0},{8,9},{9,10},{10,1... | collective-permute-start | bytes 442376 | tf_op jit(solution)/shard_map/ppermute | solution.py:19
  150.7 4.7 %copy-start.6 = (f32[2,6,24,2048]{3,2,1,0:T(8,128)S(1)}, f32[2,6,24,2048]{3,2,1,0:T(8,128)}, u32[]{:S(2)}) copy-start(f32[2,6,24,2048]{3,2,1,0:T(8,128)} %reshape.226) | copy-start | bytes 7077892
  166.5 11.5 %copy-start.2 = (f32[2,12,48,512]{3,0,2,1:T(2,128)S(1)}, f32[2,12,48,512]{3,0,2,1:T(2,128)}, u32[]{:S(2)}) copy-start(f32[2,12,48,512]{3,0,2,1:T(2,128)} %copy.172) | copy-start | bytes 7077892
  166.6 5.6 %collective-permute-start.6 = (bf16[2,12,6,512]{3,0,2,1:T(2,128)(2,1)S(1)}, bf16[2,12,6,512]{3,0,2,1:T(2,128)(2,1)S(1)}, u32[]{:S(2)}, u32[]{:S(2)}) collective-permute-start(bf16[2,12,6,512]{3,0,2,1:T(2,128)(2,1)S(1)} %slice.111), channel_id=1, source_target_pairs={{0,7},{1,0},{2,1},{3,2},{4,3},{5,4},{6,5},{7,6},{8,15},{9,8},{10,9... | collective-permute-start | bytes 442376 | tf_op jit(solution)/shard_map/ppermute | solution.py:19
  173.3 24.5 %collective-permute-start.7 = (bf16[2,3,48,512]{3,0,2,1:T(2,128)(2,1)}, bf16[2,3,48,512]{3,0,2,1:T(2,128)(2,1)}, u32[]{:S(2)}, u32[]{:S(2)}) collective-permute-start(bf16[2,3,48,512]{3,0,2,1:T(2,128)(2,1)} %pad_maximum_fusion.2), channel_id=1, source_target_pairs={{0,120},{8,0},{16,8},{24,16},{32,24},{40,32},{48,40},{56,48},{64,5... | collective-permute-start | bytes 884744 | tf_op jit(solution)/shard_map/ppermute | solution.py:19
  208.7 4.6 copy-start.23
  208.7 4.6 copy-start.29
  208.7 12.8 %slice-start = ((s8[9437184]{0:T(1024)(128)(4,1)}), s8[1048576]{0:T(1024)(128)(4,1)S(1)}, s32[]{:S(2)}) async-start(s8[9437184]{0:T(1024)(128)(4,1)} %bitcast.134), calls=%async_computation.3 | async-start | bytes 2097152
  213.3 8.2 %slice-start.1 = ((s8[9437184]{0:T(1024)(128)(4,1)}), s8[4194304]{0:T(1024)(128)(4,1)S(1)}, s32[]{:S(2)}) async-start(s8[9437184]{0:T(1024)(128)(4,1)} %bitcast.134), calls=%async_computation.4 | async-start | bytes 8388608
  213.3 8.2 %slice-start.2 = ((s8[9437184]{0:T(1024)(128)(4,1)}), s8[4194304]{0:T(1024)(128)(4,1)S(1)}, s32[]{:S(2)}) async-start(s8[9437184]{0:T(1024)(128)(4,1)} %bitcast.134), calls=%async_computation.5 | async-start | bytes 8388608
  213.3 8.2 %copy-start.17 = (bf16[8,144,1,8,64]{1,4,3,0,2:T(8,128)(2,1)S(1)}, bf16[8,144,1,8,64]{1,4,3,0,2:T(8,128)(2,1)}, u32[]{:S(2)}) copy-start(bf16[8,144,1,8,64]{1,4,3,0,2:T(8,128)(2,1)} %copy.224) | copy-start | bytes 3538948
  213.4 8.2 %copy-start.18 = (bf16[8,144,8,64]{1,3,2,0:T(8,128)(2,1)S(1)}, bf16[8,144,8,64]{1,3,2,0:T(8,128)(2,1)}, u32[]{:S(2)}) copy-start(bf16[8,144,8,64]{1,3,2,0:T(8,128)(2,1)} %copy.198) | copy-start | bytes 3538948
  227.1 6.3 %copy-start.9 = (bf16[8,144,1,8,64]{1,4,3,0,2:T(8,128)(2,1)S(1)}, bf16[8,144,1,8,64]{1,4,3,0,2:T(8,128)(2,1)}, u32[]{:S(2)}) copy-start(bf16[8,144,1,8,64]{1,4,3,0,2:T(8,128)(2,1)} %copy.225) | copy-start | bytes 3538948
  279.3 6.5 %copy-start.14 = (bf16[1152,1536]{0,1:T(8,128)(2,1)S(1)}, bf16[1152,1536]{0,1:T(8,128)(2,1)}, u32[]{:S(2)}) copy-start(bf16[1152,1536]{0,1:T(8,128)(2,1)} %convert_element_type.179) | copy-start | bytes 10616836
  279.3 6.5 %copy-start.20 = (bf16[1152,512]{1,0:T(8,128)(2,1)S(1)}, bf16[1152,512]{1,0:T(8,128)(2,1)}, u32[]{:S(2)}) copy-start(bf16[1152,512]{1,0:T(8,128)(2,1)} %convert_element_type.178) | copy-start | bytes 3538948
  298.8 6.4 %copy-start.13 = (bf16[2048,1024]{1,0:T(8,128)(2,1)S(1)}, bf16[2048,1024]{1,0:T(8,128)(2,1)}, u32[]{:S(2)}) copy-start(bf16[2048,1024]{1,0:T(8,128)(2,1)} %param.10) | copy-start | bytes 12582916
  302.5 5.8 %copy-start.10 = (f32[2,2,6,4,12,512]{5,0,4,3,2,1:T(2,128)}, f32[2,2,6,4,12,512]{5,0,4,3,2,1:T(2,128)S(1)}, u32[]{:S(2)}) copy-start(f32[2,2,6,4,12,512]{5,0,4,3,2,1:T(2,128)S(1)} %copy.208) | copy-start | bytes 7077892
  303.6 22.6 %collective-permute-start.8 = (bf16[2,3,48,512]{3,0,2,1:T(2,128)(2,1)}, bf16[2,3,48,512]{3,0,2,1:T(2,128)(2,1)}, u32[]{:S(2)}, u32[]{:S(2)}) collective-permute-start(bf16[2,3,48,512]{3,0,2,1:T(2,128)(2,1)} %slice.143), channel_id=1, source_target_pairs={{0,8},{8,16},{16,24},{24,32},{32,40},{40,48},{48,56},{56,64},{64,7... | collective-permute-start | bytes 884744 | tf_op jit(solution)/shard_map/ppermute | solution.py:19
  319.7 13.5 %all-to-all-start = ((bf16[8,2,18432]{2,1,0:T(2,128)(2,1)}), bf16[8,2,18432]{2,1,0:T(2,128)(2,1)}, u32[]{:S(2)}, u32[]{:S(2)}) async-start(bf16[8,2,18432]{2,1,0:T(2,128)(2,1)} %reshape.239), calls=%async_computation | async-start | bytes 1179648 | tf_op jit(solution)/shard_map/all_to_all | solution.py:157
  328.4 18.9 %collective-permute-start.9 = (bf16[2,12,6,512]{3,0,2,1:T(2,128)(2,1)S(1)}, bf16[2,12,6,512]{3,0,2,1:T(2,128)(2,1)}, u32[]{:S(2)}, u32[]{:S(2)}) collective-permute-start(bf16[2,12,6,512]{3,0,2,1:T(2,128)(2,1)S(1)} %fusion.35), channel_id=1, source_target_pairs={{0,1},{1,2},{2,3},{3,4},{4,5},{5,6},{6,7},{7,0},{8,9},{9,10},{10,1... | collective-permute-start | bytes 442376 | tf_op jit(solution)/shard_map/ppermute | solution.py:19
  (16 other events, 45.5 us)
Sparse Core Ops, SparseCore 0:
  289.9 158.2 all-reduce.2
where the time goes:
time: 468 us; the launch traced here: 460 us
  local copies, waits for them, and re-layouts  195 us (42%)
  waiting for transfers between devices  116 us (25%)
  matrix products  55.1 us (12%)
  other arithmetic  49.3 us (11%)
  starting transfers between devices  29.8 us (6%)
  between operations  14.9 us (3%)
    psum x1, waiting for transfers between devices, per_device(): total_qkv, total_proj = lax.psum((grad_qkv, grad_proj), ('lat', 'lon'))  94.9 us
    convert_element_type x4, local copies, waits for them, and re-layouts, attend_back(): return stacked.astype(jnp.bfloat16).reshape(win_count, length, 3 * D)  38.6 us
    unnamed x79, local copies, waits for them, and re-layouts  37 us
    ppermute x10, starting transfers between devices, from_behind(): return lax.ppermute(x, axis, [(i, (i + by) % size) for i in range(size)])  21.8 us
    ppermute x10, waiting for transfers between devices, from_behind(): return lax.ppermute(x, axis, [(i, (i + by) % size) for i in range(size)])  16.5 us
    convert_element_type x4, local copies, waits for them, and re-layouts, per_device(): grouped.reshape(levels, half_rows, half_cols, 4 * feature)  15.6 us
    convert_element_type x4, local copies, waits for them, and re-layouts, per_device(): rolled_win_f = rolled_win.astype(jnp.float32)  13.3 us
    another operation x1, local copies, waits for them, and re-layouts, split_qkv(): split_heads = qkv.reshape(win_count, length, 3, HEADS, D // HEADS)  9.56 us
  transfers between devices with their start and end apart: 13, of which 8 were waited for; matrix products, arithmetic and copies ran while one was open for 18% of the time, Pallas kernels for 0%

commit v1 on v0

v1 whole, which is shorter than its diff:
```python
import functools

import jax
import jax.numpy as jnp
import numpy as np
from jax import lax
from jax.experimental import pallas as pl
from jax.experimental.pallas import tpu as pltpu
from jax.sharding import PartitionSpec as P

D = 512
D2 = 1024
HEADS = 8
LEV = 2
WIN_LAT = 6
WIN_LON = 12
EPS = 1e-05

HALF = 288
PACK = 48
EXT = HALF + PACK
WIN = 144
TOK = 1152
CELLS = 288
BF = jnp.bfloat16
F32 = jnp.float32
MESH = pl.DeviceIdType.MESH


def one_hots():
    to_win = np.zeros((HALF, EXT), np.float32)
    pack = np.zeros((PACK, HALF), np.float32)
    for wc in range(4):
        for lr in range(6):
            for cw in range(WIN_LON):
                u = wc * 72 + lr * WIN_LON + cw
                col = WIN_LON * wc + WIN_LON // 2 + cw
                to_win[u, lr * 48 + col if col < 48 else HALF + lr * 6 + col - 48] = 1.0
    for lr in range(6):
        for c in range(6):
            pack[lr * 6 + c, lr * 48 + c] = 1.0
    return to_win, pack


def nn(a, b):
    return lax.dot_general(a, b, (((1,), (0,)), ((), ())), preferred_element_type=F32)


def nt(a, b):
    return lax.dot_general(a, b, (((1,), (1,)), ((), ())), preferred_element_type=F32)


def eye(n, scale=1.0):
    rows = lax.broadcasted_iota(jnp.int32, (n, n), 0)
    cols = lax.broadcasted_iota(jnp.int32, (n, n), 1)
    return jnp.where(rows == cols, scale, 0.0).astype(BF)


def take(ref, rows):
    return jnp.concatenate([ref[c, rows, :] for c in range(4)], 1)


def put(ref, rows, value):
    for c in range(4):
        ref[c, rows, :] = value[:, c * 128:(c + 1) * 128]


def stats(x):
    average = jnp.mean(x, -1, keepdims=True)
    centred = x - average
    variance = jnp.mean(centred * centred, -1, keepdims=True)
    return centred, lax.rsqrt(variance + EPS)


def kernel(
    tokens, region, w_qkv_h, w_proj_h, w_merge_h, d_merged, to_win_h, from_win_h, pack_h, unpack_h,
    m_out, gx_out, gw_out,
    ext, packs, wq, wp, wm, dm_raw, dm_send, dm_recv, to_win, from_win, pack, unpack,
    xw, keyw, normed, q, k, v, soft, mixed_t, mixed, tmp, b_send, b_pack, b_lat, b_packr,
    grid_s, g, d_in, d_str, d_ext, d_packs, d_win, d_qkv, merged,
    r_send, r_pack, r_lat, r_packr,
    grads, core_send, core_recv, send1, recv1, send2, recv2, send3, recv3, total,
    local_sem, halo_send, halo_recv, a2a_send, a2a_recv, ar_send, ar_recv,
):
    lat = lax.axis_index("lat")
    lon = lax.axis_index("lon")
    core = lax.rem(lat, 2)
    z_at = lax.rem(lax.div(lat, 2), 4)
    y_lo = lax.div(lat, 8)
    x_at = lax.div(lon, 2)
    y_at = lax.rem(lon, 2) * 2 + y_lo

    south = lax.rem(lat + 1, 16)
    north = lax.rem(lat + 15, 16)
    east = lax.rem(lon + 1, 8)
    west = lax.rem(lon + 7, 8)

    def on_z(by):
        return (y_lo * 8 + lax.rem(z_at + by, 4) * 2 + core, lon)

    def on_y(by):
        y_new = lax.rem(y_at + by, 4)
        return (lax.rem(y_new, 2) * 8 + z_at * 2 + core, x_at * 2 + lax.div(y_new, 2))

    def on_x(by):
        return (lat, lax.rem(x_at + by, 4) * 2 + lax.rem(lon, 2))

    def local(i, src, dst):
        copy = pltpu.make_async_copy(src, dst, local_sem.at[i])
        copy.start()
        return copy

    def remote(src, dst, sends, recvs, i, to):
        copy = pltpu.make_async_remote_copy(
            src_ref=src, dst_ref=dst, send_sem=sends.at[i], recv_sem=recvs.at[i], device_id=to, device_id_type=MESH
        )
        copy.start()
        return copy

    started = []

    loads = []
    for hb in range(4):
        for lev in range(LEV):
            rows, place = pl.ds(hb * 144, 144), pl.ds(lev * 144, 144)
            loads.append(local(len(loads), tokens.at[lev, rows], ext.at[hb, place, pl.ds(0, D)]))
            loads.append(local(len(loads), region.at[lev, rows], ext.at[hb, place, pl.ds(D, 128)]))
    for src, dst in ((pack_h, pack), (to_win_h, to_win), (d_merged, dm_raw), (w_qkv_h, wq), (w_merge_h, wm),
                     (w_proj_h, wp), (from_win_h, from_win), (unpack_h, unpack)):
        loads.append(local(len(loads), src, dst))
    grid_loads, (l_pack, l_to, l_dm, l_wq, l_wm, l_wp, l_from, l_un) = loads[:16], loads[16:]

    barrier = pltpu.get_barrier_semaphore()
    peers = [(south, lon), (north, lon), (south, east), (north, west)]
    peers += [(lat, lax.rem(lon + by, 8)) for by in range(1, 8)]
    peers += [on_z(by) for by in (1, 2, 3)] + [on_y(by) for by in (1, 3)]
    for peer in peers:
        pl.semaphore_signal(barrier, inc=1, device_id=peer, device_id_type=MESH)

    for copy in grid_loads:
        copy.wait()
    l_pack.wait()
    for hb in range(4):
        packs[hb] = nn(pack[...], ext[hb, 0:HALF, :]).astype(BF)
    pl.semaphore_wait(barrier, len(peers))

    def send_halo(full, small, base):
        out = [remote(full.at[0, pl.ds(0, HALF)], full.at[4, pl.ds(0, HALF)], halo_send, halo_recv, base, (north, lon))]
        for hb in range(4):
            to = (north, west) if hb == 0 else (lat, west)
            out.append(remote(small.at[hb], full.at[hb if hb else 4, pl.ds(HALF, PACK)], halo_send, halo_recv, base + 1 + hb, to))
        started.extend(out)
        return out

    halo = send_halo(ext, packs, 0)

    l_dm.wait()
    for s in range(8):
        part = dm_raw[:, s * 24:(s + 1) * 24, :].astype(F32)
        dm_send[s] = part.reshape(CELLS, 128).astype(BF)
    mine = pl.ds(pl.multiple_of(lon * 128, 128), 128)
    a2a_in = []
    for by in range(1, 8):
        to = lax.rem(lon + by, 8)
        a2a_in.append(remote(dm_send.at[to], dm_recv.at[:, mine], a2a_send, a2a_recv, by - 1, (lat, to)))
    started.extend(a2a_in)
    dm_recv[:, mine] = dm_send[lon]

    l_to.wait()
    l_wq.wait()
    for copy in halo:
        copy.wait_recv()
    for half in range(4):
        moved = nn(to_win[...], ext[half + 1])
        for wc in range(4):
            at = ((half // 2) * 4 + wc) * WIN + (half % 2) * 72
            xw[at:at + 72, :] = moved[wc * 72:(wc + 1) * 72, :D]
            keyw[at:at + 72, :] = moved[wc * 72:(wc + 1) * 72, D:]

    def norm_window(w, _):
        rows = pl.ds(pl.multiple_of(w * WIN, WIN), WIN)
        centred, inverse = stats(xw[rows, :])
        normed[rows, :] = (centred * inverse).astype(BF)
        return 0

    lax.fori_loop(0, 8, norm_window, 0)

    def project_band(band, _):
        rows = pl.ds(pl.multiple_of(band * 576, 576), 576)
        block = normed[rows, :]
        q[rows, :] = (nn(block, wq[:, 0:D]).astype(BF) * 0.125).astype(BF)
        k[rows, :] = nn(block, wq[:, D:2 * D]).astype(BF)
        v[rows, :] = nn(block, wq[:, 2 * D:3 * D]).astype(BF)
        return 0

    lax.fori_loop(0, 2, project_band, 0)

    lane = lax.broadcasted_iota(jnp.int32, (WIN, 128), 1)
    low = lane < 64

    def attend(w, _):
        rows = pl.ds(pl.multiple_of(w * WIN, WIN), WIN)
        hot = jnp.where(keyw[rows, :] == lane.astype(F32), 1.0, 0.0).astype(BF)
        bias = (nt(hot, hot) - 1.0) * 1e30
        v_t = nt(eye(D), v[rows, :]).astype(BF)
        for pair in range(4):
            cols = slice(pair * 128, (pair + 1) * 128)
            q_p, k_p = q[rows, cols], k[rows, cols]
            for side in range(2):
                head = pair * 2 + side
                k_m = jnp.where(low if side == 0 else ~low, k_p, jnp.zeros_like(k_p))
                raw = jnp.exp(nt(k_m, q_p) + bias)
                total_w = jnp.sum(raw, 0, keepdims=True)
                shrink = jnp.where(total_w > 1.0, 2.0 ** -32, 1.0)
                part = (raw * shrink) * (1.0 / (total_w * shrink))
                soft[w, head] = part
                mixed_t[w, head * 64:(head + 1) * 64, :] = nn(v_t[head * 64:(head + 1) * 64, :], part.astype(BF)).astype(BF)
        mixed[rows, :] = nt(eye(WIN), mixed_t[w]).astype(BF)
        return 0

    lax.fori_loop(0, 8, attend, 0)

    l_wp.wait()
    l_from.wait()
    l_un.wait()

    def to_grid(half, base, lat_send, lat_recv, pack_send, pack_recv, keep):
        first = (half // 2) * 4
        block = jnp.concatenate([tmp[(first + wc) * WIN + (half % 2) * 72:(first + wc) * WIN + (half % 2) * 72 + 72, :] for wc in range(4)], 0)
        moved = nn(from_win[...], block.astype(BF))
        pack_send[half] = moved[HALF:, :].astype(BF)
        out = []
        if half == 3:
            lat_send[...] = moved[:HALF, :].astype(BF)
            out.append(remote(lat_send, lat_recv, halo_send, halo_recv, base, (south, lon)))
            out.append(remote(pack_send.at[3], pack_recv.at[0], halo_send, halo_recv, base + 1, (south, east)))
        else:
            put(keep, slice((half + 1) * HALF, (half + 2) * HALF), moved[:HALF, :])
            out.append(remote(pack_send.at[half], pack_recv.at[half + 1], halo_send, halo_recv, base + 2 + half, (lat, east)))
        started.extend(out)
        return out

    def project_branch(i, _):
        rows = pl.ds(pl.multiple_of((1 - i) * 576, 576), 576)
        tmp[rows, :] = nn(mixed[rows, :], wp[...])
        return 0

    lax.fori_loop(0, 2, project_branch, 0)
    branch_halo = []
    for half in (3, 2, 1, 0):
        branch_halo += to_grid(half, 5, b_send, b_lat, b_pack, b_packr, grid_s)

    l_wm.wait()
    for copy in a2a_in:
        copy.wait_recv()

    def d_in_part(p, _):
        d_in[p] = nt(dm_recv[...], wm[pl.ds(pl.multiple_of(p * D, D), D), :])
        return 0

    lax.fori_loop(0, 4, d_in_part, 0)

    for copy in branch_halo:
        copy.wait_recv()
    for hb in range(4):
        at = slice(hb * HALF, (hb + 1) * HALF)
        own = b_lat[...].astype(F32) if hb == 0 else take(grid_s, at)
        full = own + nn(unpack[...], b_packr[hb])
        put(grid_s, at, (ext[hb, 0:HALF, 0:D].astype(F32) + full).astype(BF).astype(F32))

    def cell_rows(p, lev, i):
        row = 2 * i + p % 2
        return ((row // 3 * 2 + lev) * 3 + row % 3) * 48 + p // 2

    for p in range(4):
        for lev in range(LEV):
            for i in range(6):
                at = (lev * 6 + i) * 24
                g[p, at:at + 24, :] = take(grid_s, pl.ds(cell_rows(p, lev, i), 24, stride=2))

    average = sum(jnp.sum(g[p], -1, keepdims=True) for p in range(4)) / (4 * D)
    variance = 0.0
    for p in range(4):
        centred = g[p] - average
        variance = variance + jnp.sum(centred * centred, -1, keepdims=True)
    inverse = lax.rsqrt(variance / (4 * D) + EPS)
    mean_d = sum(jnp.sum(d_in[p], -1, keepdims=True) for p in range(4)) / (4 * D)
    mean_dh = sum(jnp.sum(d_in[p] * ((g[p] - average) * inverse), -1, keepdims=True) for p in range(4)) / (4 * D)
    for p in range(4):
        hat = (g[p] - average) * inverse
        d_part = inverse * (d_in[p] - mean_d - hat * mean_dh)
        g[p] = hat
        for lev in range(LEV):
            for i in range(6):
                at = (lev * 6 + i) * 24
                put(d_str, pl.ds(cell_rows(p, lev, i), 24, stride=2), d_part[at:at + 24, :])

    for hb in range(4):
        d_ext[hb, 0:HALF, :] = take(d_str, slice(hb * HALF, (hb + 1) * HALF)).astype(BF)
    for hb in range(4):
        d_packs[hb] = nn(pack[...], d_ext[hb, 0:HALF, :]).astype(BF)
    d_halo = send_halo(d_ext, d_packs, 10)

    for n in range(2):
        cols = slice(n * 512, (n + 1) * 512)
        sums = nn(g[0].astype(BF), wm[0:D, cols])
        for p in range(1, 4):
            sums = sums + nn(g[p].astype(BF), wm[p * D:(p + 1) * D, cols])
        for s in range(4):
            merged[n * 4 + s] = sums[:, s * 128:(s + 1) * 128].astype(BF)
    for by in range(1, 8):
        to = lax.rem(lon + by, 8)
        started.append(remote(merged.at[to], m_out.at[lon], a2a_send, a2a_recv, 6 + by, (lat, to)))
    merged_out = started[-7:]
    merged_own = local(36, merged.at[lon], m_out.at[lon])

    for copy in d_halo:
        copy.wait_recv()
    for half in range(4):
        moved = nn(to_win[...], d_ext[half + 1])
        for wc in range(4):
            at = ((half // 2) * 4 + wc) * WIN + (half % 2) * 72
            tmp[at:at + 72, :] = moved[wc * 72:(wc + 1) * 72, :]

    d_mix = mixed

    def back_band(band, _):
        rows = pl.ds(pl.multiple_of(band * 576, 576), 576)
        block = tmp[rows, :].astype(BF)
        d_win[rows, :] = block
        d_mix[rows, :] = nt(block, wp[...]).astype(BF)
        return 0

    lax.fori_loop(0, 2, back_band, 0)

    grads[0] = jnp.zeros((D, D), F32)

    def proj_window(w, _):
        rows = pl.ds(pl.multiple_of(w * WIN, WIN), WIN)
        grads[0] = grads[0] + nn(mixed_t[w], d_win[rows, :])
        return 0

    lax.fori_loop(0, 8, proj_window, 0)

    def attend_back(w, _):
        rows = pl.ds(pl.multiple_of(w * WIN, WIN), WIN)
        k_t = nt(eye(D, 0.125), k[rows, :]).astype(BF)
        parts = []
        for pair in range(4):
            cols = slice(pair * 128, (pair + 1) * 128)
            q_p, v_p, dm_p = q[rows, cols], v[rows, cols], d_mix[rows, cols]
            d_v, d_k = [], []
            for side in range(2):
                head = pair * 2 + side
                part = soft[w, head]
                v_m = jnp.where(low if side == 0 else ~low, v_p, jnp.zeros_like(v_p))
                d_soft = nt(v_m, dm_p)
                delta = jnp.sum(part * d_soft, 0, keepdims=True)
                d_s = (part * (d_soft - delta)).astype(BF)
                d_v.append(nn(part.astype(BF), dm_p))
                d_k.append(nn(d_s, q_p))
                parts.append(nn(k_t[head * 64:(head + 1) * 64, :], d_s).astype(BF))
            d_qkv[rows, D + pair * 128:D + (pair + 1) * 128] = jnp.where(low, d_k[0], d_k[1]).astype(BF)
            d_qkv[rows, 2 * D + pair * 128:2 * D + (pair + 1) * 128] = jnp.where(low, d_v[0], d_v[1]).astype(BF)
        d_qkv[rows, 0:D] = nt(eye(WIN), jnp.concatenate(parts, 0)).astype(BF)
        return 0

    lax.fori_loop(0, 8, attend_back, 0)

    def norm_back_band(band, _):
        rows = pl.ds(pl.multiple_of(band * 576, 576), 576)
        d_norm = nt(d_qkv[rows, :], wq[...])
        centred, inverse = stats(xw[rows, :])
        hat = centred * inverse
        tmp[rows, :] = inverse * (
            d_norm - jnp.mean(d_norm, -1, keepdims=True) - hat * jnp.mean(d_norm * hat, -1, keepdims=True)
        )
        return 0

    lax.fori_loop(0, 2, norm_back_band, 0)
    roll_halo = []
    for half in (3, 2, 1, 0):
        roll_halo += to_grid(half, 15, r_send, r_lat, r_pack, r_packr, grid_s)

    normed_t = jnp.concatenate([nt(eye(D), normed[i * 384:(i + 1) * 384, :]).astype(BF) for i in range(3)], 1)
    for m in range(3):
        grads[m + 1] = nn(normed_t, d_qkv[:, m * D:(m + 1) * D])

    orders = (("z", "y", "x"), ("y", "x", "z"), ("x", "z", "y"), ("z", "x", "y"))
    along = {"z": (on_z, z_at), "y": (on_y, y_at), "x": (on_x, x_at)}
    acc1 = d_in
    other = (lat + 1 - 2 * core, lon)
    half_at = pl.multiple_of(core * 256, 256)
    away_at = pl.multiple_of((1 - core) * 256, 256)
    ar = [[None] * 4 for _ in range(4)]
    for m in range(4):
        core_send[m] = grads[m, pl.ds(away_at, 256), :].astype(BF)
        ar[m][0] = [remote(core_send.at[m], core_recv.at[m], ar_send, ar_recv, m * 20, other)]
    for m in range(4):
        move, at = along[orders[m][0]]
        ar[m][0][0].wait_recv()
        acc1[m, 0:256, :] = grads[m, pl.ds(half_at, 256), :] + core_recv[m].astype(F32)
        send1[m] = acc1[m, 0:256, :].astype(BF)
        ar[m][1] = []
        for by in range(1, 4):
            rows = pl.ds(pl.multiple_of(lax.rem(at + by, 4) * 64, 64), 64)
            ar[m][1].append(remote(send1.at[m, rows], recv1.at[m, by - 1], ar_send, ar_recv, m * 20 + by, move(by)))
    places = []
    for m in range(4):
        at = along[orders[m][0]][1]
        for copy in ar[m][1]:
            copy.wait_recv()
        own = acc1[m, pl.ds(pl.multiple_of(at * 64, 64), 64), :]
        for j in range(3):
            own = own + recv1[m, j].astype(F32)
        send2[m] = own.astype(BF)
        acc1[m, 0:64, :] = own
        move, at2 = along[orders[m][1]]
        ar[m][2] = []
        for by in range(1, 4):
            rows = pl.ds(pl.multiple_of(lax.rem(at2 + by, 4) * 16, 16), 16)
            ar[m][2].append(remote(send2.at[m, rows], recv2.at[m, by - 1], ar_send, ar_recv, m * 20 + 3 + by, move(by)))
    for m in range(4):
        at2 = along[orders[m][1]][1]
        for copy in ar[m][2]:
            copy.wait_recv()
        own = acc1[m, pl.ds(pl.multiple_of(at2 * 16, 16), 16), :]
        for j in range(3):
            own = own + recv2[m, j].astype(F32)
        send3[m] = own.astype(BF)
        acc1[m, 0:16, :] = own
        move, at3 = along[orders[m][2]]
        ar[m][3] = []
        for by in range(1, 4):
            cols = pl.ds(pl.multiple_of(lax.rem(at3 + by, 4) * 128, 128), 128)
            ar[m][3].append(remote(send3.at[m, :, cols], recv3.at[m, by - 1], ar_send, ar_recv, m * 20 + 6 + by, move(by)))
    factor = float(LEV * 192 * 384) ** -0.5
    gather = []
    for m in range(4):
        ats = [along[axis][1] for axis in orders[m]]
        for copy in ar[m][3]:
            copy.wait_recv()
        cols = pl.ds(pl.multiple_of(ats[2] * 128, 128), 128)
        own = acc1[m, 0:16, cols]
        for j in range(3):
            own = own + recv3[m, j].astype(F32)
        row1 = core * 256
        row2 = row1 + ats[0] * 64
        row3 = row2 + ats[1] * 16
        rows3 = pl.ds(pl.multiple_of(row3, 16), 16)
        total[m, rows3, cols] = (own * factor).astype(BF)
        move = along[orders[m][2]][0]
        gather.append([
            remote(total.at[m, rows3, cols], total.at[m, rows3, cols], ar_send, ar_recv, m * 20 + 9 + by, move(by))
            for by in range(1, 4)
        ])
        places.append((pl.ds(pl.multiple_of(row1, 256), 256), pl.ds(pl.multiple_of(row2, 64), 64), rows3))
    gather2 = []
    for m in range(4):
        for copy in gather[m]:
            copy.wait_recv()
        move, rows = along[orders[m][1]][0], places[m][2]
        gather2.append([
            remote(total.at[m, rows], total.at[m, rows], ar_send, ar_recv, m * 20 + 12 + by, move(by))
            for by in range(1, 4)
        ])
    gather3 = []
    for m in range(4):
        for copy in gather2[m]:
            copy.wait_recv()
        move, rows = along[orders[m][0]][0], places[m][1]
        gather3.append([
            remote(total.at[m, rows], total.at[m, rows], ar_send, ar_recv, m * 20 + 15 + by, move(by))
            for by in range(1, 4)
        ])

    for copy in roll_halo:
        copy.wait_recv()
    outs = []
    for hb in range(4):
        at = slice(hb * HALF, (hb + 1) * HALF)
        own = r_lat[...].astype(F32) if hb == 0 else take(grid_s, at)
        put(d_str, at, take(d_str, at) + own + nn(unpack[...], r_packr[hb]))
        for lev in range(LEV):
            for c in range(4):
                src = d_str.at[c, pl.ds(hb * HALF + lev * 144, 144)]
                outs.append(local(len(outs), src, gx_out.at[lev, pl.ds(hb * 144, 144), pl.ds(c * 128, 128)]))

    gather4 = []
    for m in range(4):
        for copy in gather3[m]:
            copy.wait_recv()
        rows = places[m][0]
        gather4.append(remote(total.at[m, rows], total.at[m, rows], ar_send, ar_recv, m * 20 + 19, other))
    for m in range(4):
        gather4[m].wait_recv()
        outs.append(local(len(outs), total.at[m], gw_out.at[m]))

    for copy in merged_out:
        copy.wait_recv()
    for copy in started:
        copy.wait_send()
    for m in range(4):
        for stage in ar[m] + [gather[m], gather2[m], gather3[m], [gather4[m]]]:
            for copy in stage:
                copy.wait_send()
    merged_own.wait()
    for copy in outs:
        copy.wait()


def vmem(*shape, dtype=BF):
    return pltpu.VMEM(shape, dtype)


SCRATCH = [
    vmem(5, EXT, 640), vmem(4, PACK, 640), vmem(D, 3 * D), vmem(D, D), vmem(4 * D, D2),
    vmem(12, 192, 128), vmem(8, CELLS, 128), vmem(CELLS, D2), vmem(HALF, EXT), vmem(EXT, HALF), vmem(PACK, HALF), vmem(HALF, PACK),
    vmem(TOK, D, dtype=F32), vmem(TOK, 128, dtype=F32), vmem(TOK, D), vmem(TOK, D), vmem(TOK, D), vmem(TOK, D),
    vmem(8, HEADS, WIN, WIN, dtype=F32), vmem(8, D, WIN), vmem(TOK, D), vmem(TOK, D, dtype=F32),
    vmem(HALF, D), vmem(4, PACK, D), vmem(HALF, D), vmem(4, PACK, D),
    vmem(4, TOK, 128, dtype=F32), vmem(4, CELLS, D, dtype=F32), vmem(4, CELLS, D, dtype=F32), vmem(4, TOK, 128, dtype=F32),
    vmem(5, EXT, D), vmem(4, PACK, D), vmem(TOK, D), vmem(TOK, 3 * D), vmem(8, CELLS, 128),
    vmem(HALF, D), vmem(4, PACK, D), vmem(HALF, D), vmem(4, PACK, D),
    vmem(4, D, D, dtype=F32), vmem(4, 256, D), vmem(4, 256, D), vmem(4, 256, D),
    vmem(4, 3, 64, D), vmem(4, 64, D), vmem(4, 3, 16, D), vmem(4, 16, D), vmem(4, 3, 16, 128), vmem(4, D, D),
    pltpu.SemaphoreType.DMA((37,)), pltpu.SemaphoreType.DMA((20,)), pltpu.SemaphoreType.DMA((20,)),
    pltpu.SemaphoreType.DMA((14,)), pltpu.SemaphoreType.DMA((14,)),
    pltpu.SemaphoreType.DMA((80,)), pltpu.SemaphoreType.DMA((80,)),
]


def per_device(tokens, region, w_qkv, w_proj, w_merge, d_merged):
    levels, lat_rows, lon_cols, feature = tokens.shape
    rows = jnp.arange(lat_rows, dtype=jnp.int32)
    edge = jnp.where((lax.axis_index("lat") == 0) & (rows < WIN_LAT // 2), 4, 0)
    keys = (region + edge[:, None]).astype(BF)
    keys = jnp.broadcast_to(keys[None, :, :, None], (levels, lat_rows, lon_cols, 128))
    to_win, pack = one_hots()
    consts = [jnp.asarray(a, BF) for a in (to_win, to_win.T, pack, pack.T)]
    anywhere = pl.BlockSpec(memory_space=pl.ANY)
    m_out, gx_out, gw_out = pl.pallas_call(
        kernel,
        out_shape=(
            jax.ShapeDtypeStruct((8, CELLS, 128), BF),
            jax.ShapeDtypeStruct((levels, 576, feature), F32),
            jax.ShapeDtypeStruct((4, D, D), BF),
        ),
        in_specs=[anywhere] * 10,
        out_specs=(anywhere,) * 3,
        scratch_shapes=SCRATCH,
        compiler_params=pltpu.CompilerParams(
            collective_id=0, has_side_effects=True, vmem_limit_bytes=64 * 1024 * 1024
        ),
    )(
        tokens.reshape(levels, 576, feature), keys.reshape(levels, 576, 128), w_qkv, w_proj, w_merge,
        d_merged.reshape(12, 192, 128), *consts,
    )
    merged = m_out.reshape(8, levels, 6, 24, 128).transpose(1, 2, 0, 3, 4).reshape(levels, 6, 192, 128)
    grad_x = gx_out.reshape(levels, lat_rows, lon_cols, feature)
    grad_qkv = jnp.concatenate([gw_out[1], gw_out[2], gw_out[3]], 1).astype(F32)
    return (merged, grad_x, grad_qkv, gw_out[0].astype(F32))


def solution(mesh):
    in_specs = (
        P(None, "lat", "lon", None),
        P("lat", "lon"),
        P(),
        P(),
        P(),
        P(None, "lat", None, "lon"),
    )
    out_specs = (P(None, "lat", None, "lon"), P(None, "lat", "lon", None), P(), P())
    return jax.shard_map(
        per_device, mesh=mesh, in_specs=in_specs, out_specs=out_specs, check_vma=False
    )
```

time: 468 us -> 136 us (0.29); the launches traced: 460 us -> 136 us
  local copies, waits for them, and re-layouts: 195 us -> 4.6 us
  Pallas kernels: 0 us -> 125 us
  waiting for transfers between devices: 116 us -> 0 us
  matrix products: 55.1 us -> 0 us
  other arithmetic: 49.3 us -> 5.63 us
  starting transfers between devices: 29.8 us -> 0 us
  between operations: 14.9 us -> 0.66 us
    pallas_call x0 -> x1, Pallas kernels: none -> 125 us  [per_device(): pl.pallas_call(kernel, out_shape=(jax.ShapeDtypeStruct((8, CELLS, 128), B...]
    psum x1 -> x0, waiting for transfers between devices: 94.9 us -> none  [per_device(): total_qkv, total_proj = lax.psum((grad_qkv, grad_proj), ('lat', 'lon'))]
    convert_element_type x16 -> x0, local copies, waits for them, and re-layouts: 76.1 us -> none  [the longest x4 38.6 us: attend_back(): return stacked.astype(jnp.bfloat16).reshape(win_count, length, 3 * D)]
    dot_general x14 -> x0, matrix products: 55.1 us -> none  [the longest x1 8.2 us: attend_back(): jnp.einsum('whqk,wqhd->wkhd', soft_bf, grad_heads, preferred_element_type...]
    unnamed x79 -> x3, local copies, waits for them, and re-layouts: 37 us -> 1.68 us
    another operation x6 -> x0, local copies, waits for them, and re-layouts: 25.9 us -> none  [the longest x1 9.56 us: split_qkv(): split_heads = qkv.reshape(win_count, length, 3, HEADS, D // HEADS)]
    ppermute x10 -> x0, starting transfers between devices: 21.8 us -> none  [from_behind(): return lax.ppermute(x, axis, [(i, (i + by) % size) for i in range(size)])]
    ppermute x10 -> x0, waiting for transfers between devices: 16.5 us -> none  [from_behind(): return lax.ppermute(x, axis, [(i, (i + by) % size) for i in range(size)])]
  transfers between devices with their start and end apart: 13 -> 0, of which waited for: 8 -> 0; matrix products, arithmetic and copies ran while one was open for 18% -> 0% of each run, Pallas kernels for 0% -> 0%
where the time goes in v1:
time: 136 us
  Pallas kernels  125 us (92%)
  other arithmetic  5.63 us (4%)
  local copies, waits for them, and re-layouts  4.6 us (3%)
    pallas_call x1, Pallas kernels, per_device(): pl.pallas_call(kernel, out_shape=(jax.ShapeDtypeStruct((8, CELLS, 128), B...  125 us
    convert_element_type x1, other arithmetic, per_device(): return (merged, grad_x, grad_qkv, gw_out[0].astype(F32))  2.78 us

profile of v1, /device:TPU:1, one launch (start us, length us, event | category | flops | bytes accessed | tf_op | source)
XLA Modules:
  0.0 135.6 jit_solution(10835760952954074935)
XLA Ops:
  0.6 0.8 add_convert_fusion
  1.4 0.1 broadcast_in_dim.19
  1.5 0.9 broadcast_in_dim.20.region
  2.4 124.8 %shard_map.129 = (bf16[8,288,128]{2,1,0:T(8,128)(2,1)}, f32[2,576,512]{2,1,0:T(8,128)}, bf16[4,512,512]{2,1,0:T(8,128)(2,1)}) custom-call(bf16[2,576,512]{2,1,0:T(8,128)(2,1)} %bitcast.17, bf16[2,576,128]{2,1,0:T(8,128)(2,1)} %broadcast_in_dim.20.region, bf16[512,1536]{1,0:T(8,128)(2,1)} %w_qkv_h.1, bf16[512,512]{1,0:T(8,128)(2,1)} %w_proj_h.1, ...), custom_call_target="tpu_custom_call" | custom-call | tf_op jit(solution)/shard_map/pallas_call | solution.py:542
  127.1 2.0 %copy.14 = bf16[2,6,8,24,128]{4,3,2,1,0:T(8,128)(2,1)} copy(bf16[2,6,8,24,128]{4,3,1,0,2:T(8,128)(2,1)} %bitcast.20) | data formatting | bytes 1179648 | tf_op jit(solution)/shard_map/transpose | solution.py:559
  129.1 2.8 %bitcast_convert_fusion = (f32[512,512]{1,0:T(8,128)}, bf16[512,512]{1,0:T(8,128)(2,1)S(1)}, bf16[512,512]{1,0:T(8,128)(2,1)S(1)}, bf16[512,512]{1,0:T(8,128)(2,1)S(1)}) fusion(bf16[4,512,512]{2,1,0:T(8,128)(2,1)} %get-tuple-element.9), kind=kLoop, calls=%fused_computation.1 | loop fusion | flops 262144 | bytes 4718592 | tf_op jit(solution)/shard_map/convert_element_type | solution.py:562
  131.9 0.0 copy-start
  131.9 2.1 %maximum_convert_fusion = f32[512,1536]{1,0:T(8,128)} fusion(bf16[512,512]{1,0:T(8,128)(2,1)S(1)} %get-tuple-element.11, bf16[512,512]{1,0:T(8,128)(2,1)S(1)} %get-tuple-element.12, bf16[512,512]{1,0:T(8,128)(2,1)S(1)} %get-tuple-element.13), kind=kLoop, calls=%fused_computation | loop fusion | flops 4718592 | bytes 4718592 | tf_op jit(solution)/shard_map/convert_element_type | solution.py:561
  134.0 0.3 copy-done
  134.2 1.4 %copy.16 = f32[2,12,48,512]{3,2,1,0:T(8,128)} copy(f32[2,12,48,512]{3,2,1,0:T(8,128)S(1)} %bitcast.16) | data formatting | bytes 4718592
  (1 shorter events, 0.0 us)
Async XLA Ops:
  131.9 2.4 %copy-start = (f32[2,576,512]{2,1,0:T(8,128)S(1)}, f32[2,576,512]{2,1,0:T(8,128)}, u32[]{:S(2)}) copy-start(f32[2,576,512]{2,1,0:T(8,128)} %get-tuple-element.8) | copy-start | bytes 7077892

commit v2 on v1

v2 whole, which is shorter than its diff:
```python
import functools

import jax
import jax.numpy as jnp
import numpy as np
from jax import lax
from jax.experimental import pallas as pl
from jax.experimental.pallas import tpu as pltpu
from jax.sharding import PartitionSpec as P

D = 512
D2 = 1024
HEADS = 8
LEV = 2
WIN_LAT = 6
WIN_LON = 12
EPS = 1e-05

HALF = 288
PACK = 48
EXT = HALF + PACK
WIN = 144
TOK = 1152
CELLS = 288
BF = jnp.bfloat16
F32 = jnp.float32
MESH = pl.DeviceIdType.MESH


CHUNK_LANE = (0, 0, 128, 256, 256)
SEGMENTS = []
for _head in range(HEADS):
    _at = _head * WIN
    while _at < (_head + 1) * WIN:
        _end = min((_at // 256 + 1) * 256, (_head + 1) * WIN)
        SEGMENTS.append((_head, _at, _end))
        _at = _end


def one_hots():
    to_win = np.zeros((HALF, EXT), np.float32)
    pack = np.zeros((PACK, HALF), np.float32)
    for wc in range(4):
        for lr in range(6):
            for cw in range(WIN_LON):
                u = wc * 72 + lr * WIN_LON + cw
                col = WIN_LON * wc + WIN_LON // 2 + cw
                to_win[u, lr * 48 + col if col < 48 else HALF + lr * 6 + col - 48] = 1.0
    for lr in range(6):
        for c in range(6):
            pack[lr * 6 + c, lr * 48 + c] = 1.0
    return to_win, pack


def nn(a, b):
    return lax.dot_general(a, b, (((1,), (0,)), ((), ())), preferred_element_type=F32)


def nt(a, b):
    return lax.dot_general(a, b, (((1,), (1,)), ((), ())), preferred_element_type=F32)


def tn(a, b):
    return lax.dot_general(a, b, (((0,), (0,)), ((), ())), preferred_element_type=F32)


def take(ref, rows):
    return jnp.concatenate([ref[c, rows, :] for c in range(4)], 1)


def put(ref, rows, value):
    for c in range(4):
        ref[c, rows, :] = value[:, c * 128:(c + 1) * 128]


def stats(x):
    average = jnp.mean(x, -1, keepdims=True)
    centred = x - average
    variance = jnp.mean(centred * centred, -1, keepdims=True)
    return centred, lax.rsqrt(variance + EPS)


def kernel(
    tokens, region, w_qkv_h, w_proj_h, w_merge_h, d_merged, to_win_h, from_win_h, pack_h, unpack_h,
    m_out, gx_out, gq_out, gp_out,
    ext, packs, regions, wq, wp, wm, dm_raw, dm_send, dm_recv, to_win, from_win, pack, unpack,
    xw, keyw, normed, q, k, v, block_q, block_d, staged, soft, mixed_t, normed_t, mixed, tmp, b_send, b_pack, b_lat, b_packr,
    grid_s, g, d_in, d_str, d_ext, d_packs, d_win, d_mix, d_qkv, merged, merged_in, merged_all,
    r_send, r_pack, r_lat, r_packr,
    grads, core_send, core_recv, send1, recv1, send2, recv2, send3, recv3, total,
    local_sem, halo_send, halo_recv, a2a_send, a2a_recv, ar_send, ar_recv,
):
    lat = lax.axis_index("lat")
    lon = lax.axis_index("lon")
    core = lax.rem(lat, 2)
    z_at = lax.rem(lax.div(lat, 2), 4)
    y_lo = lax.div(lat, 8)
    x_at = lax.div(lon, 2)
    y_at = lax.rem(lon, 2) * 2 + y_lo

    south = lax.rem(lat + 1, 16)
    north = lax.rem(lat + 15, 16)
    east = lax.rem(lon + 1, 8)
    west = lax.rem(lon + 7, 8)

    def on_z(by):
        return (y_lo * 8 + lax.rem(z_at + by, 4) * 2 + core, lon)

    def on_y(by):
        y_new = lax.rem(y_at + by, 4)
        return (lax.rem(y_new, 2) * 8 + z_at * 2 + core, x_at * 2 + lax.div(y_new, 2))

    def on_x(by):
        return (lat, lax.rem(x_at + by, 4) * 2 + lax.rem(lon, 2))

    def local(i, src, dst):
        copy = pltpu.make_async_copy(src, dst, local_sem.at[i])
        copy.start()
        return copy

    def remote(src, dst, sends, recvs, i, to):
        copy = pltpu.make_async_remote_copy(
            src_ref=src, dst_ref=dst, send_sem=sends.at[i], recv_sem=recvs.at[i], device_id=to, device_id_type=MESH
        )
        copy.start()
        return copy

    started = []

    loads = []
    for hb in range(4):
        for lev in range(LEV):
            rows, place = pl.ds(hb * 144, 144), pl.ds(lev * 144, 144)
            loads.append(local(len(loads), tokens.at[lev, rows], ext.at[hb, place, pl.ds(0, D)]))
    for src, dst in ((region, regions), (pack_h, pack), (to_win_h, to_win), (d_merged, dm_raw), (w_qkv_h, wq), (w_merge_h, wm),
                     (w_proj_h, wp), (from_win_h, from_win), (unpack_h, unpack)):
        loads.append(local(len(loads), src, dst))
    grid_loads, (l_reg, l_pack, l_to, l_dm, l_wq, l_wm, l_wp, l_from, l_un) = loads[:8], loads[8:]

    barrier = pltpu.get_barrier_semaphore()
    peers = [(south, lon), (north, lon), (south, east), (north, west)]
    peers += [(lat, lax.rem(lon + by, 8)) for by in range(1, 8)]
    peers += [on_z(by) for by in (1, 2, 3)] + [on_y(by) for by in (1, 3)]
    for peer in peers:
        pl.semaphore_signal(barrier, inc=1, device_id=peer, device_id_type=MESH)

    for copy in grid_loads:
        copy.wait()
    l_reg.wait()
    corner = lax.broadcasted_iota(jnp.int32, (48, 48), 0) == lax.broadcasted_iota(jnp.int32, (48, 48), 1)
    for row in range(12):
        column = jnp.sum(jnp.where(corner, regions[row:row + 1, :].astype(F32), 0.0), 1, keepdims=True)
        if row < WIN_LAT // 2:
            column = column + jnp.where(lat == 0, 4.0, 0.0)
        for lev in range(LEV):
            at = lev * 144 + row % 3 * 48
            ext[row // 3, at:at + 48, D:] = jnp.broadcast_to(column, (48, 128)).astype(BF)
    l_pack.wait()
    for hb in range(4):
        packs[hb] = nn(pack[...], ext[hb, 0:HALF, :]).astype(BF)
    pl.semaphore_wait(barrier, len(peers))

    def send_halo(full, small, base):
        out = [remote(full.at[0, pl.ds(0, HALF)], full.at[4, pl.ds(0, HALF)], halo_send, halo_recv, base, (north, lon))]
        for hb in range(4):
            to = (north, west) if hb == 0 else (lat, west)
            out.append(remote(small.at[hb], full.at[hb if hb else 4, pl.ds(HALF, PACK)], halo_send, halo_recv, base + 1 + hb, to))
        started.extend(out)
        return out

    halo = send_halo(ext, packs, 0)

    l_dm.wait()
    for s in range(8):
        part = dm_raw[:, s * 24:(s + 1) * 24, :].astype(F32)
        dm_send[s] = part.reshape(CELLS, 128).astype(BF)
    mine = pl.ds(pl.multiple_of(lon * 128, 128), 128)
    a2a_in = []
    for by in range(1, 8):
        to = lax.rem(lon + by, 8)
        a2a_in.append(remote(dm_send.at[to], dm_recv.at[:, mine], a2a_send, a2a_recv, by - 1, (lat, to)))
    started.extend(a2a_in)
    dm_recv[:, mine] = dm_send[lon]

    def window_rows(half, first, moved, wide):
        for i in range(moved.shape[0] // 72):
            at = ((half // 2) * 4 + first + i) * WIN + (half % 2) * 72
            wide[at:at + 72, :] = moved[i * 72:(i + 1) * 72, :D]
            if moved.shape[1] > D:
                keyw[at:at + 72, :] = moved[i * 72:(i + 1) * 72, D:]

    def norm_window(w, _):
        rows = pl.ds(pl.multiple_of(w * WIN, WIN), WIN)
        centred, inverse = stats(xw[rows, :])
        normed[rows, :] = (centred * inverse).astype(BF)
        return 0

    def project_pair(i, _):
        rows = pl.ds(pl.multiple_of(i * 288, 288), 288)
        block = normed[rows, :]
        q[rows, :] = (nn(block, wq[:, 0:D]).astype(BF) * 0.125).astype(BF)
        k[rows, :] = nn(block, wq[:, D:2 * D]).astype(BF)
        v[rows, :] = nn(block, wq[:, 2 * D:3 * D]).astype(BF)
        return 0

    lane = lax.broadcasted_iota(jnp.int32, (WIN, 128), 1)
    low = lane < 64

    def spread(ref, rows, src, filler):
        blank = jnp.zeros((WIN, 128), BF)
        for head, first, last in SEGMENTS:
            chunk, at = first // 256, pl.ds(first, last - first)
            part = slice(first - head * WIN, last - head * WIN)
            own = src[rows, (head // 2) * 128:(head // 2 + 1) * 128]
            own = jnp.where(low if head % 2 == 0 else ~low, own, blank)
            block = head // 2 - CHUNK_LANE[chunk] // 128
            fill = blank if filler is None else filler
            if chunk == 0:
                ref[at, 0:128] = own[part]
                ref[at, 128:256] = fill[part]
            else:
                ref[at, 0:128] = (jnp.where(low, fill, own) if block == 0 else fill)[part]
                ref[at, 128:256] = (own if block == 1 else blank)[part]

    def by_heads(stage, left, right, chunk):
        out = tn(left, right[:, CHUNK_LANE[chunk]:CHUNK_LANE[chunk] + 256])
        for head, first, last in SEGMENTS:
            if first // 256 == chunk:
                block = head // 2 - CHUNK_LANE[chunk] // 128
                rows = slice(first - chunk * 256, last - chunk * 256)
                stage[first:last, :] = out[rows, block * 128:(block + 1) * 128]

    def joined(stage, pair):
        even, odd = 2 * pair * WIN, (2 * pair + 1) * WIN
        return jnp.where(low, stage[even:even + WIN, :], stage[odd:odd + WIN, :])

    def attend(w, q_b, stage):
        rows = pl.ds(pl.multiple_of(w * WIN, WIN), WIN)
        same = keyw[rows, :] == lane.astype(F32)
        differ = jnp.where(same | ~low, 0.0, 1.0).astype(BF)
        forbid = jnp.where(same, -1e30, 0.0).astype(BF)
        spread(q_b, rows, q, differ)
        k_b = [k[rows, i * 128:(i + 1) * 128] for i in range(4)]
        k_x = [jnp.concatenate([k_b[0], jnp.where(low, forbid, k_b[1])], 1)]
        k_x += [jnp.concatenate([jnp.where(low, forbid, k_b[i]), k_b[i + 1]], 1) for i in range(3)]
        values = v[rows, :]
        for chunk in range(5):
            cols = slice(chunk * 256, min(chunk * 256 + 256, 1152))
            raw = jnp.exp(nt(k_x[min(chunk, 3)], q_b[cols, :]))
            total_w = jnp.sum(raw, 0, keepdims=True)
            shrink = jnp.where(total_w > 1.0, 2.0 ** -32, 1.0)
            part = (raw * shrink) * (1.0 / (total_w * shrink))
            soft[w, :, cols] = part
            by_heads(stage, part.astype(BF), values, chunk)
        for pair in range(4):
            mixed[rows, pair * 128:(pair + 1) * 128] = joined(stage, pair).astype(BF)

    def attend_pair(i, _):
        attend(2 * i, block_q.at[0], staged.at[0])
        attend(2 * i + 1, block_q.at[1], staged.at[1])
        return 0

    l_to.wait()
    for half in range(2):
        window_rows(half, 0, nn(to_win[0:WIN, 0:HALF], ext[half + 1, 0:HALF, :]), xw)
    lax.fori_loop(0, 2, norm_window, 0)
    l_wq.wait()
    project_pair(0, 0)
    attend_pair(0, 0)

    for copy in halo:
        copy.wait_recv()
    for half in range(2):
        window_rows(half, 2, nn(to_win[WIN:, :], ext[half + 1]), xw)
    for half in range(2, 4):
        window_rows(half, 0, nn(to_win[...], ext[half + 1]), xw)
    lax.fori_loop(2, 8, norm_window, 0)
    lax.fori_loop(1, 4, project_pair, 0)
    lax.fori_loop(2, 4, attend_pair, 0)

    l_wp.wait()
    l_from.wait()
    l_un.wait()

    def to_grid(half, base, lat_send, lat_recv, pack_send, pack_recv, keep):
        first = (half // 2) * 4
        block = jnp.concatenate([tmp[(first + wc) * WIN + (half % 2) * 72:(first + wc) * WIN + (half % 2) * 72 + 72, :] for wc in range(4)], 0)
        moved = nn(from_win[...], block.astype(BF))
        pack_send[half] = moved[HALF:, :].astype(BF)
        out = []
        if half == 3:
            lat_send[...] = moved[:HALF, :].astype(BF)
            out.append(remote(lat_send, lat_recv, halo_send, halo_recv, base, (south, lon)))
            out.append(remote(pack_send.at[3], pack_recv.at[0], halo_send, halo_recv, base + 1, (south, east)))
        else:
            put(keep, slice((half + 1) * HALF, (half + 2) * HALF), moved[:HALF, :])
            out.append(remote(pack_send.at[half], pack_recv.at[half + 1], halo_send, halo_recv, base + 2 + half, (lat, east)))
        started.extend(out)
        return out

    branch_halo = []
    for band in (1, 0):
        if band == 0:
            attend_pair(1, 0)
        rows = slice(band * 576, (band + 1) * 576)
        tmp[rows, :] = nn(mixed[rows, :], wp[...])
        for half in (band * 2 + 1, band * 2):
            branch_halo += to_grid(half, 5, b_send, b_lat, b_pack, b_packr, grid_s)

    l_wm.wait()
    for copy in a2a_in:
        copy.wait_recv()

    def d_in_part(p, _):
        d_in[p] = nt(dm_recv[...], wm[pl.ds(pl.multiple_of(p * D, D), D), :])
        return 0

    lax.fori_loop(0, 4, d_in_part, 0)
    for i in range(9):
        rows = slice(i * 128, (i + 1) * 128)
        normed_t[:, rows] = normed[rows, :].T
        mixed_t[:, rows] = mixed[rows, :].T

    for copy in branch_halo:
        copy.wait_recv()
    for hb in range(4):
        at = slice(hb * HALF, (hb + 1) * HALF)
        own = b_lat[...].astype(F32) if hb == 0 else take(grid_s, at)
        full = own + nn(unpack[...], b_packr[hb])
        put(grid_s, at, (ext[hb, 0:HALF, 0:D].astype(F32) + full).astype(BF).astype(F32))

    def cell_rows(p, lev, i):
        row = 2 * i + p % 2
        return ((row // 3 * 2 + lev) * 3 + row % 3) * 48 + p // 2

    for p in range(4):
        for lev in range(LEV):
            for i in range(6):
                at = (lev * 6 + i) * 24
                g[p, at:at + 24, :] = take(grid_s, pl.ds(cell_rows(p, lev, i), 24, stride=2))

    average = sum(jnp.sum(g[p], -1, keepdims=True) for p in range(4)) / (4 * D)
    variance = 0.0
    for p in range(4):
        centred = g[p] - average
        variance = variance + jnp.sum(centred * centred, -1, keepdims=True)
    inverse = lax.rsqrt(variance / (4 * D) + EPS)
    mean_d = sum(jnp.sum(d_in[p], -1, keepdims=True) for p in range(4)) / (4 * D)
    mean_dh = sum(jnp.sum(d_in[p] * ((g[p] - average) * inverse), -1, keepdims=True) for p in range(4)) / (4 * D)
    for p in range(4):
        hat = (g[p] - average) * inverse
        d_part = inverse * (d_in[p] - mean_d - hat * mean_dh)
        g[p] = hat
        for lev in range(LEV):
            for i in range(6):
                at = (lev * 6 + i) * 24
                put(d_str, pl.ds(cell_rows(p, lev, i), 24, stride=2), d_part[at:at + 24, :])

    for hb in range(4):
        d_ext[hb, 0:HALF, :] = take(d_str, slice(hb * HALF, (hb + 1) * HALF)).astype(BF)
    for hb in range(4):
        d_packs[hb] = nn(pack[...], d_ext[hb, 0:HALF, :]).astype(BF)
    d_halo = send_halo(d_ext, d_packs, 10)

    for n in range(2):
        cols = slice(n * 512, (n + 1) * 512)
        sums = nn(g[0].astype(BF), wm[0:D, cols])
        for p in range(1, 4):
            sums = sums + nn(g[p].astype(BF), wm[p * D:(p + 1) * D, cols])
        for s in range(4):
            merged[n * 4 + s] = sums[:, s * 128:(s + 1) * 128].astype(BF)
    for by in range(1, 8):
        to = lax.rem(lon + by, 8)
        started.append(remote(merged.at[to], merged_in.at[lon], a2a_send, a2a_recv, 6 + by, (lat, to)))
    merged_out = started[-7:]
    merged_in[lon] = merged[lon]

    def back_pair(i, _):
        rows = pl.ds(pl.multiple_of(i * 288, 288), 288)
        block = tmp[rows, :].astype(BF)
        d_win[rows, :] = block
        d_mix[rows, :] = nt(block, wp[...]).astype(BF)
        return 0

    def attend_back(w, q_b, d_b, stage):
        rows = pl.ds(pl.multiple_of(w * WIN, WIN), WIN)
        spread(q_b, rows, q, None)
        spread(d_b, rows, d_mix, None)
        keys, values = k[rows, :], v[rows, :]
        d_k, d_v = [], []
        for chunk in range(5):
            cols = slice(chunk * 256, min(chunk * 256 + 256, 1152))
            part = soft[w, :, cols]
            d_soft = nt(values[:, CHUNK_LANE[chunk]:CHUNK_LANE[chunk] + 256], d_b[cols, :])
            delta = jnp.sum(part * d_soft, 0, keepdims=True)
            d_s = (part * (d_soft - delta)).astype(BF)
            d_v.append(nn(part.astype(BF), d_b[cols, :]))
            d_k.append(nn(d_s, q_b[cols, :]))
            by_heads(stage, d_s, keys, chunk)
        for which, d in ((1, d_k), (2, d_v)):
            both = [d[0][:, 0:128] + d[1][:, 0:128], d[1][:, 128:256] + d[2][:, 0:128],
                    d[2][:, 128:256] + d[3][:, 0:128] + d[4][:, 0:128], d[3][:, 128:256] + d[4][:, 128:256]]
            for pair in range(4):
                d_qkv[rows, which * D + pair * 128:which * D + (pair + 1) * 128] = both[pair].astype(BF)
        for pair in range(4):
            d_qkv[rows, pair * 128:(pair + 1) * 128] = (joined(stage, pair) * 0.125).astype(BF)

    def attend_back_pair(i, _):
        attend_back(2 * i, block_q.at[0], block_d.at[0], staged.at[0])
        attend_back(2 * i + 1, block_q.at[1], block_d.at[1], staged.at[1])
        return 0

    orders = (("z", "y", "x"), ("y", "x", "z"), ("x", "z", "y"), ("z", "x", "y"))
    along = {"z": (on_z, z_at), "y": (on_y, y_at), "x": (on_x, x_at)}
    acc1 = d_in
    other = (lat + 1 - 2 * core, lon)
    half_at = pl.multiple_of(core * 256, 256)
    away_at = pl.multiple_of((1 - core) * 256, 256)
    factor = float(LEV * 192 * 384) ** -0.5
    outs = []

    def summed(m):
        (move1, at1), (move2, at2), (move3, at3) = [along[axis] for axis in orders[m]]

        def send(i, src, dst, to):
            copy = remote(src, dst, ar_send, ar_recv, m * 20 + i, to)
            started.append(copy)
            return copy

        core_send[m] = grads[m, pl.ds(away_at, 256), :].astype(BF)
        flying = [send(0, core_send.at[m], core_recv.at[m], other)]
        yield
        flying[0].wait_recv()
        acc1[m, 0:256, :] = grads[m, pl.ds(half_at, 256), :] + core_recv[m].astype(F32)
        send1[m] = acc1[m, 0:256, :].astype(BF)
        flying = []
        for by in range(1, 4):
            rows = pl.ds(pl.multiple_of(lax.rem(at1 + by, 4) * 64, 64), 64)
            flying.append(send(by, send1.at[m, rows], recv1.at[m, by - 1], move1(by)))
        yield
        for copy in flying:
            copy.wait_recv()
        own = acc1[m, pl.ds(pl.multiple_of(at1 * 64, 64), 64), :]
        for j in range(3):
            own = own + recv1[m, j].astype(F32)
        send2[m] = own.astype(BF)
        acc1[m, 0:64, :] = own
        flying = []
        for by in range(1, 4):
            rows = pl.ds(pl.multiple_of(lax.rem(at2 + by, 4) * 16, 16), 16)
            flying.append(send(3 + by, send2.at[m, rows], recv2.at[m, by - 1], move2(by)))
        yield
        for copy in flying:
            copy.wait_recv()
        own = acc1[m, pl.ds(pl.multiple_of(at2 * 16, 16), 16), :]
        for j in range(3):
            own = own + recv2[m, j].astype(F32)
        send3[m] = own.astype(BF)
        acc1[m, 0:16, :] = own
        flying = []
        for by in range(1, 4):
            cols = pl.ds(pl.multiple_of(lax.rem(at3 + by, 4) * 128, 128), 128)
            flying.append(send(6 + by, send3.at[m, :, cols], recv3.at[m, by - 1], move3(by)))
        yield
        for copy in flying:
            copy.wait_recv()
        cols = pl.ds(pl.multiple_of(at3 * 128, 128), 128)
        own = acc1[m, 0:16, cols]
        for j in range(3):
            own = own + recv3[m, j].astype(F32)
        row1 = core * 256
        row2 = row1 + at1 * 64
        row3 = row2 + at2 * 16
        rows1, rows2, rows3 = [pl.ds(pl.multiple_of(r, n), n) for r, n in ((row1, 256), (row2, 64), (row3, 16))]
        total[m, rows3, cols] = (own * factor).astype(BF)
        flying = [send(9 + by, total.at[m, rows3, cols], total.at[m, rows3, cols], move3(by)) for by in range(1, 4)]
        yield
        for copy in flying:
            copy.wait_recv()
        flying = [send(12 + by, total.at[m, rows3], total.at[m, rows3], move2(by)) for by in range(1, 4)]
        yield
        for copy in flying:
            copy.wait_recv()
        flying = [send(15 + by, total.at[m, rows2], total.at[m, rows2], move1(by)) for by in range(1, 4)]
        yield
        for copy in flying:
            copy.wait_recv()
        flying = [send(19, total.at[m, rows1], total.at[m, rows1], other)]
        yield
        flying[0].wait_recv()
        outs.append(local(m, total.at[m], gq_out.at[:, pl.ds((m - 1) * D, D)] if m else gp_out))
        yield

    for half in range(2):
        window_rows(half, 0, nn(to_win[0:WIN, 0:HALF], d_ext[half + 1, 0:HALF, :]), tmp)
    back_pair(0, 0)
    attend_back_pair(0, 0)
    for copy in d_halo:
        copy.wait_recv()
    for half in range(2):
        window_rows(half, 2, nn(to_win[WIN:, :], d_ext[half + 1]), tmp)
    for half in range(2, 4):
        window_rows(half, 0, nn(to_win[...], d_ext[half + 1]), tmp)
    lax.fori_loop(1, 4, back_pair, 0)
    grads[0] = nn(mixed_t[...], d_win[...])
    sums = [summed(0)]
    next(sums[0])
    for i in (1, 2, 3):
        attend_back_pair(i, 0)
        next(sums[0])

    for m in range(3):
        grads[m + 1] = nn(normed_t[...], d_qkv[:, m * D:(m + 1) * D])
        sums.append(summed(m + 1))
        next(sums[m + 1])

    def norm_back_band(band, _):
        rows = pl.ds(pl.multiple_of(band * 576, 576), 576)
        d_norm = nt(d_qkv[rows, :], wq[...])
        centred, inverse = stats(xw[rows, :])
        hat = centred * inverse
        tmp[rows, :] = inverse * (
            d_norm - jnp.mean(d_norm, -1, keepdims=True) - hat * jnp.mean(d_norm * hat, -1, keepdims=True)
        )
        return 0

    roll_halo = []
    for band in (1, 0):
        norm_back_band(band, 0)
        for half in (band * 2 + 1, band * 2):
            roll_halo += to_grid(half, 15, r_send, r_lat, r_pack, r_packr, grid_s)
        for step in sums:
            next(step)

    for copy in merged_out:
        copy.wait_recv()
    for s in range(8):
        merged_all[:, s * 24:(s + 1) * 24, :] = merged_in[s].astype(F32).reshape(12, 24, 128)
    dm_raw[...] = merged_all[...].astype(BF)
    outs.append(local(4, dm_raw, m_out))
    for step in sums:
        next(step)

    for copy in roll_halo:
        copy.wait_recv()
    for hb in range(4):
        at = slice(hb * HALF, (hb + 1) * HALF)
        own = r_lat[...].astype(F32) if hb == 0 else take(grid_s, at)
        put(d_str, at, take(d_str, at) + own + nn(unpack[...], r_packr[hb]))
        for lev in range(LEV):
            for c in range(4):
                src = d_str.at[c, pl.ds(hb * HALF + lev * 144, 144)]
                to = gx_out.at[lev, pl.ds(hb * 144, 144), pl.ds(c * 128, 128)]
                outs.append(local(5 + hb * 8 + lev * 4 + c, src, to))
        for step in sums:
            next(step, None)
    for _ in range(8):
        for step in sums:
            next(step, None)

    for copy in started:
        copy.wait_send()
    for copy in outs:
        copy.wait()


def vmem(*shape, dtype=BF):
    return pltpu.VMEM(shape, dtype)


SCRATCH = [
    vmem(5, EXT, 640), vmem(4, PACK, 640), vmem(12, 48, dtype=jnp.int32), vmem(D, 3 * D), vmem(D, D), vmem(4 * D, D2),
    vmem(12, 192, 128), vmem(8, CELLS, 128), vmem(CELLS, D2), vmem(HALF, EXT), vmem(EXT, HALF), vmem(PACK, HALF), vmem(HALF, PACK),
    vmem(TOK, D, dtype=F32), vmem(TOK, 128, dtype=F32), vmem(TOK, D), vmem(TOK, D), vmem(TOK, D), vmem(TOK, D),
    vmem(2, 1152, 256), vmem(2, 1152, 256), vmem(2, 1152, 128, dtype=F32), vmem(8, WIN, 1152, dtype=F32), vmem(D, TOK), vmem(D, TOK), vmem(TOK, D), vmem(TOK, D, dtype=F32),
    vmem(HALF, D), vmem(4, PACK, D), vmem(HALF, D), vmem(4, PACK, D),
    vmem(4, TOK, 128, dtype=F32), vmem(4, CELLS, D, dtype=F32), vmem(4, CELLS, D, dtype=F32), vmem(4, TOK, 128, dtype=F32),
    vmem(5, EXT, D), vmem(4, PACK, D), vmem(TOK, D), vmem(TOK, D), vmem(TOK, 3 * D), vmem(8, CELLS, 128), vmem(8, CELLS, 128), vmem(12, 192, 128, dtype=F32),
    vmem(HALF, D), vmem(4, PACK, D), vmem(HALF, D), vmem(4, PACK, D),
    vmem(4, D, D, dtype=F32), vmem(4, 256, D), vmem(4, 256, D), vmem(4, 256, D),
    vmem(4, 3, 64, D), vmem(4, 64, D), vmem(4, 3, 16, D), vmem(4, 16, D), vmem(4, 3, 16, 128), vmem(4, D, D),
    pltpu.SemaphoreType.DMA((38,)), pltpu.SemaphoreType.DMA((20,)), pltpu.SemaphoreType.DMA((20,)),
    pltpu.SemaphoreType.DMA((14,)), pltpu.SemaphoreType.DMA((14,)),
    pltpu.SemaphoreType.DMA((80,)), pltpu.SemaphoreType.DMA((80,)),
]


def per_device(tokens, region, w_qkv, w_proj, w_merge, d_merged):
    levels, lat_rows, lon_cols, feature = tokens.shape
    to_win, pack = one_hots()
    consts = [jnp.asarray(a, BF) for a in (to_win, to_win.T, pack, pack.T)]
    anywhere = pl.BlockSpec(memory_space=pl.ANY)
    m_out, gx_out, gq_out, gp_out = pl.pallas_call(
        kernel,
        out_shape=(
            jax.ShapeDtypeStruct((12, 192, 128), BF),
            jax.ShapeDtypeStruct((levels, 576, feature), F32),
            jax.ShapeDtypeStruct((D, 3 * D), BF),
            jax.ShapeDtypeStruct((D, D), BF),
        ),
        in_specs=[anywhere] * 10,
        out_specs=(anywhere,) * 4,
        scratch_shapes=SCRATCH,
        compiler_params=pltpu.CompilerParams(
            collective_id=0, has_side_effects=True, vmem_limit_bytes=64 * 1024 * 1024
        ),
    )(
        tokens.reshape(levels, 576, feature), region, w_qkv, w_proj, w_merge,
        d_merged.reshape(12, 192, 128), *consts,
    )
    merged = m_out.reshape(levels, 6, 192, 128)
    grad_x = gx_out.reshape(levels, lat_rows, lon_cols, feature)
    return (merged, grad_x, gq_out.astype(F32), gp_out.astype(F32))


def solution(mesh):
    in_specs = (
        P(None, "lat", "lon", None),
        P("lat", "lon"),
        P(),
        P(),
        P(),
        P(None, "lat", None, "lon"),
    )
    out_specs = (P(None, "lat", None, "lon"), P(None, "lat", "lon", None), P(), P())
    return jax.shard_map(
        per_device, mesh=mesh, in_specs=in_specs, out_specs=out_specs, check_vma=False
    )
```

time: 136 us -> 113 us (0.83)
  Pallas kernels: 125 us -> 105 us
  local copies, waits for them, and re-layouts: 4.6 us -> 2.35 us
    pallas_call x1, Pallas kernels: 125 us -> 105 us  [per_device(): pl.pallas_call(kernel, out_shape=(jax.ShapeDtypeStruct((12, 192, 128), BF...]
    transpose x1 -> x0, local copies, waits for them, and re-layouts: 1.96 us -> none  [per_device(): m_out.reshape(8, levels, 6, 24, 128).transpose(1, 2, 0, 3, 4)]
    convert_element_type x3 -> x2, other arithmetic: 5.62 us -> 4.67 us  [per_device(): return (merged, grad_x, gq_out.astype(F32), gp_out.astype(F32))]
where the time goes in v2:
time: 113 us
  Pallas kernels  105 us (93%)
  other arithmetic  4.67 us (4%)
  local copies, waits for them, and re-layouts  2.35 us (2%)
    pallas_call x1, Pallas kernels, per_device(): pl.pallas_call(kernel, out_shape=(jax.ShapeDtypeStruct((12, 192, 128), BF...  105 us
    convert_element_type x2, other arithmetic, per_device(): return (merged, grad_x, gq_out.astype(F32), gp_out.astype(F32))  4.67 us
    unnamed x8, local copies, waits for them, and re-layouts  2.35 us

profile of v2, /device:TPU:1, one launch (start us, length us, event | category | flops | bytes accessed | tf_op | source)
XLA Modules:
  0.0 112.8 jit_solution(18270030888456049970)
XLA Ops:
  0.6 105.1 %shard_map.129 = (bf16[12,192,128]{2,1,0:T(8,128)(2,1)}, f32[2,576,512]{2,1,0:T(8,128)}, bf16[512,1536]{1,0:T(8,128)(2,1)}, bf16[512,512]{1,0:T(8,128)(2,1)}) custom-call(bf16[2,576,512]{2,1,0:T(8,128)(2,1)} %bitcast.5, s32[12,48]{1,0:T(8,128)} %region.1, bf16[512,1536]{1,0:T(8,128)(2,1)} %w_qkv_h.1, bf16[512,512]{1,0:T(8,128)(2,1)} %w_proj_h.1, ...), custom_call_target="tpu_custom_call" | custom-call | tf_op jit(solution)/shard_map/pallas_call | solution.py:593
  105.7 0.0 copy-start.2
  105.7 0.0 copy-start.1
  105.7 3.6 %convert_element_type.6 = f32[512,1536]{1,0:T(8,128)} convert(bf16[512,1536]{1,0:T(8,128)(2,1)} %get-tuple-element.10) | non-fusion elementwise | flops 786432 | bytes 4718592 | tf_op jit(solution)/shard_map/convert_element_type | solution.py:613
  109.3 0.0 copy-start
  109.3 0.0 copy-done.2
  109.3 1.1 convert_element_type.7
  110.4 0.0 copy-done.1
  110.4 0.8 copy.16
  111.2 0.1 copy-done
  111.4 1.4 %copy.17 = f32[2,12,48,512]{3,2,1,0:T(8,128)} copy(f32[2,12,48,512]{3,2,1,0:T(8,128)S(1)} %bitcast.4) | data formatting | bytes 4718592
Async XLA Ops:
  105.7 3.6 %copy-start.2 = (bf16[512,512]{1,0:T(8,128)(2,1)S(1)}, bf16[512,512]{1,0:T(8,128)(2,1)}, u32[]{:S(2)}) copy-start(bf16[512,512]{1,0:T(8,128)(2,1)} %get-tuple-element.11) | copy-start | bytes 1572868
  105.7 4.7 %copy-start.1 = (bf16[12,192,128]{2,1,0:T(8,128)(2,1)S(1)}, bf16[12,192,128]{2,1,0:T(8,128)(2,1)}, u32[]{:S(2)}) copy-start(bf16[12,192,128]{2,1,0:T(8,128)(2,1)} %get-tuple-element.8) | copy-start | bytes 1769476
  109.3 2.0 %copy-start = (f32[2,576,512]{2,1,0:T(8,128)S(1)}, f32[2,576,512]{2,1,0:T(8,128)}, u32[]{:S(2)}) copy-start(f32[2,576,512]{2,1,0:T(8,128)} %get-tuple-element.9) | copy-start | bytes 7077892

commit v3 on v2

--- a/solution.py
+++ b/solution.py
@@ -87,7 +87,7 @@
     xw, keyw, normed, q, k, v, block_q, block_d, staged, soft, mixed_t, normed_t, mixed, tmp, b_send, b_pack, b_lat, b_packr,
     grid_s, g, d_in, d_str, d_ext, d_packs, d_win, d_mix, d_qkv, merged, merged_in, merged_all,
     r_send, r_pack, r_lat, r_packr,
-    grads, core_send, core_recv, send1, recv1, send2, recv2, send3, recv3, total,
+    grads, core_send, core_recv, send1, recv1, send2, recv2, total,
     local_sem, halo_send, halo_recv, a2a_send, a2a_recv, ar_send, ar_recv,
 ):
     lat = lax.axis_index("lat")
@@ -103,15 +103,23 @@
     east = lax.rem(lon + 1, 8)
     west = lax.rem(lon + 7, 8)
 
+    places = {"x": x_at, "y": y_at, "z": z_at}
+
+    def moved_by(steps):
+        x, y, z = [lax.rem(places[axis] + steps[axis], 4) if steps.get(axis) else places[axis] for axis in "xyz"]
+        return (lax.rem(y, 2) * 8 + z * 2 + core, x * 2 + lax.div(y, 2))
+
     def on_z(by):
-        return (y_lo * 8 + lax.rem(z_at + by, 4) * 2 + core, lon)
+        return moved_by({"z": by})
 
     def on_y(by):
-        y_new = lax.rem(y_at + by, 4)
-        return (lax.rem(y_new, 2) * 8 + z_at * 2 + core, x_at * 2 + lax.div(y_new, 2))
+        return moved_by({"y": by})
 
     def on_x(by):
-        return (lat, lax.rem(x_at + by, 4) * 2 + lax.rem(lon, 2))
+        return moved_by({"x": by})
+
+    def on_plane(order, b2, b3):
+        return moved_by({order[1]: b2, order[2]: b3})
 
     def local(i, src, dst):
         copy = pltpu.make_async_copy(src, dst, local_sem.at[i])
@@ -141,6 +149,11 @@
     peers = [(south, lon), (north, lon), (south, east), (north, west)]
     peers += [(lat, lax.rem(lon + by, 8)) for by in range(1, 8)]
     peers += [on_z(by) for by in (1, 2, 3)] + [on_y(by) for by in (1, 3)]
+    for first, second in ("xy", "yz", "xz"):
+        for b2 in range(1, 4):
+            for b3 in range(1, 4):
+                if (first, second, b3) != ("x", "y", 2):
+                    peers.append(moved_by({first: b2, second: b3}))
     for peer in peers:
         pl.semaphore_signal(barrier, inc=1, device_id=peer, device_id_type=MESH)
 
@@ -174,14 +187,6 @@
     for s in range(8):
         part = dm_raw[:, s * 24:(s + 1) * 24, :].astype(F32)
         dm_send[s] = part.reshape(CELLS, 128).astype(BF)
-    mine = pl.ds(pl.multiple_of(lon * 128, 128), 128)
-    a2a_in = []
-    for by in range(1, 8):
-        to = lax.rem(lon + by, 8)
-        a2a_in.append(remote(dm_send.at[to], dm_recv.at[:, mine], a2a_send, a2a_recv, by - 1, (lat, to)))
-    started.extend(a2a_in)
-    dm_recv[:, mine] = dm_send[lon]
-
     def window_rows(half, first, moved, wide):
         for i in range(moved.shape[0] // 72):
             at = ((half // 2) * 4 + first + i) * WIN + (half % 2) * 72
@@ -270,6 +275,13 @@
 
     for copy in halo:
         copy.wait_recv()
+    mine = pl.ds(pl.multiple_of(lon * 128, 128), 128)
+    a2a_in = []
+    for by in range(1, 8):
+        to = lax.rem(lon + by, 8)
+        a2a_in.append(remote(dm_send.at[to], dm_recv.at[:, mine], a2a_send, a2a_recv, by - 1, (lat, to)))
+    started.extend(a2a_in)
+    dm_recv[:, mine] = dm_send[lon]
     for half in range(2):
         window_rows(half, 2, nn(to_win[WIN:, :], ext[half + 1]), xw)
     for half in range(2, 4):
@@ -369,12 +381,6 @@
             sums = sums + nn(g[p].astype(BF), wm[p * D:(p + 1) * D, cols])
         for s in range(4):
             merged[n * 4 + s] = sums[:, s * 128:(s + 1) * 128].astype(BF)
-    for by in range(1, 8):
-        to = lax.rem(lon + by, 8)
-        started.append(remote(merged.at[to], merged_in.at[lon], a2a_send, a2a_recv, 6 + by, (lat, to)))
-    merged_out = started[-7:]
-    merged_in[lon] = merged[lon]
-
     def back_pair(i, _):
         rows = pl.ds(pl.multiple_of(i * 288, 288), 288)
         block = tmp[rows, :].astype(BF)
@@ -420,10 +426,10 @@
     outs = []
 
     def summed(m):
-        (move1, at1), (move2, at2), (move3, at3) = [along[axis] for axis in orders[m]]
+        (move1, at1), (_, at2), (_, at3) = [along[axis] for axis in orders[m]]
 
         def send(i, src, dst, to):
-            copy = remote(src, dst, ar_send, ar_recv, m * 20 + i, to)
+            copy = remote(src, dst, ar_send, ar_recv, m * 38 + i, to)
             started.append(copy)
             return copy
 
@@ -445,50 +451,38 @@
             own = own + recv1[m, j].astype(F32)
         send2[m] = own.astype(BF)
         acc1[m, 0:64, :] = own
+        rest = [(b2, b3) for b2 in range(4) for b3 in range(4) if (b2, b3) != (0, 0)]
         flying = []
-        for by in range(1, 4):
-            rows = pl.ds(pl.multiple_of(lax.rem(at2 + by, 4) * 16, 16), 16)
-            flying.append(send(3 + by, send2.at[m, rows], recv2.at[m, by - 1], move2(by)))
+        for i, (b2, b3) in enumerate(rest):
+            rows = pl.ds(pl.multiple_of(lax.rem(at2 + b2, 4) * 16, 16), 16)
+            cols = pl.ds(pl.multiple_of(lax.rem(at3 + b3, 4) * 128, 128), 128)
+            flying.append(send(4 + i, send2.at[m, rows, cols], recv2.at[m, i], on_plane(orders[m], b2, b3)))
         yield
         for copy in flying:
             copy.wait_recv()
-        own = acc1[m, pl.ds(pl.multiple_of(at2 * 16, 16), 16), :]
-        for j in range(3):
-            own = own + recv2[m, j].astype(F32)
-        send3[m] = own.astype(BF)
-        acc1[m, 0:16, :] = own
-        flying = []
-        for by in range(1, 4):
-            cols = pl.ds(pl.multiple_of(lax.rem(at3 + by, 4) * 128, 128), 128)
-            flying.append(send(6 + by, send3.at[m, :, cols], recv3.at[m, by - 1], move3(by)))
-        yield
-        for copy in flying:
-            copy.wait_recv()
-        cols = pl.ds(pl.multiple_of(at3 * 128, 128), 128)
-        own = acc1[m, 0:16, cols]
-        for j in range(3):
-            own = own + recv3[m, j].astype(F32)
         row1 = core * 256
         row2 = row1 + at1 * 64
         row3 = row2 + at2 * 16
         rows1, rows2, rows3 = [pl.ds(pl.multiple_of(r, n), n) for r, n in ((row1, 256), (row2, 64), (row3, 16))]
+        cols = pl.ds(pl.multiple_of(at3 * 128, 128), 128)
+        own = acc1[m, pl.ds(pl.multiple_of(at2 * 16, 16), 16), cols]
+        for j in range(15):
+            own = own + recv2[m, j].astype(F32)
         total[m, rows3, cols] = (own * factor).astype(BF)
-        flying = [send(9 + by, total.at[m, rows3, cols], total.at[m, rows3, cols], move3(by)) for by in range(1, 4)]
+        piece = total.at[m, rows3, cols]
+        flying = [send(19 + i, piece, piece, on_plane(orders[m], b2, b3)) for i, (b2, b3) in enumerate(rest)]
         yield
         for copy in flying:
             copy.wait_recv()
-        flying = [send(12 + by, total.at[m, rows3], total.at[m, rows3], move2(by)) for by in range(1, 4)]
+        flying = [send(33 + by, total.at[m, rows2], total.at[m, rows2], move1(by)) for by in range(1, 4)]
         yield
         for copy in flying:
             copy.wait_recv()
-        flying = [send(15 + by, total.at[m, rows2], total.at[m, rows2], move1(by)) for by in range(1, 4)]
-        yield
-        for copy in flying:
-            copy.wait_recv()
-        flying = [send(19, total.at[m, rows1], total.at[m, rows1], other)]
+        flying = [send(37, total.at[m, rows1], total.at[m, rows1], other)]
         yield
         flying[0].wait_recv()
-        outs.append(local(m, total.at[m], gq_out.at[:, pl.ds((m - 1) * D, D)] if m else gp_out))
+        grads[m] = total[m].astype(F32)
+        outs.append(local(m, grads.at[m], gq_out.at[:, pl.ds((m - 1) * D, D)] if m else gp_out))
         yield
 
     for half in range(2):
@@ -497,6 +491,11 @@
     attend_back_pair(0, 0)
     for copy in d_halo:
         copy.wait_recv()
+    for by in range(1, 8):
+        to = lax.rem(lon + by, 8)
+        started.append(remote(merged.at[to], merged_in.at[lon], a2a_send, a2a_recv, 6 + by, (lat, to)))
+    merged_out = started[-7:]
+    merged_in[lon] = merged[lon]
     for half in range(2):
         window_rows(half, 2, nn(to_win[WIN:, :], d_ext[half + 1]), tmp)
     for half in range(2, 4):
@@ -507,7 +506,8 @@
     next(sums[0])
     for i in (1, 2, 3):
         attend_back_pair(i, 0)
-        next(sums[0])
+        if i != 2:
+            next(sums[0])
 
     for m in range(3):
         grads[m + 1] = nn(normed_t[...], d_qkv[:, m * D:(m + 1) * D])
@@ -578,10 +578,10 @@
     vmem(5, EXT, D), vmem(4, PACK, D), vmem(TOK, D), vmem(TOK, D), vmem(TOK, 3 * D), vmem(8, CELLS, 128), vmem(8, CELLS, 128), vmem(12, 192, 128, dtype=F32),
     vmem(HALF, D), vmem(4, PACK, D), vmem(HALF, D), vmem(4, PACK, D),
     vmem(4, D, D, dtype=F32), vmem(4, 256, D), vmem(4, 256, D), vmem(4, 256, D),
-    vmem(4, 3, 64, D), vmem(4, 64, D), vmem(4, 3, 16, D), vmem(4, 16, D), vmem(4, 3, 16, 128), vmem(4, D, D),
+    vmem(4, 3, 64, D), vmem(4, 64, D), vmem(4, 15, 16, 128), vmem(4, D, D),
     pltpu.SemaphoreType.DMA((38,)), pltpu.SemaphoreType.DMA((20,)), pltpu.SemaphoreType.DMA((20,)),
     pltpu.SemaphoreType.DMA((14,)), pltpu.SemaphoreType.DMA((14,)),
-    pltpu.SemaphoreType.DMA((80,)), pltpu.SemaphoreType.DMA((80,)),
+    pltpu.SemaphoreType.DMA((152,)), pltpu.SemaphoreType.DMA((152,)),
 ]
 
 
@@ -595,8 +595,8 @@
         out_shape=(
             jax.ShapeDtypeStruct((12, 192, 128), BF),
             jax.ShapeDtypeStruct((levels, 576, feature), F32),
-            jax.ShapeDtypeStruct((D, 3 * D), BF),
-            jax.ShapeDtypeStruct((D, D), BF),
+            jax.ShapeDtypeStruct((D, 3 * D), F32),
+            jax.ShapeDtypeStruct((D, D), F32),
         ),
         in_specs=[anywhere] * 10,
         out_specs=(anywhere,) * 4,
@@ -610,7 +610,7 @@
     )
     merged = m_out.reshape(levels, 6, 192, 128)
     grad_x = gx_out.reshape(levels, lat_rows, lon_cols, feature)
-    return (merged, grad_x, gq_out.astype(F32), gp_out.astype(F32))
+    return (merged, grad_x, gq_out, gp_out)
 
 
 def solution(mesh):

time: 113 us -> 112 us (level)
  local copies, waits for them, and re-layouts: 2.35 us -> 8.39 us
  other arithmetic: 4.67 us -> 0 us
  Pallas kernels: 105 us -> 103 us
    unnamed x8, local copies, waits for them, and re-layouts: 2.35 us -> 8.39 us
    convert_element_type x2 -> x0, other arithmetic: 4.67 us -> none  [per_device(): return (merged, grad_x, gq_out.astype(F32), gp_out.astype(F32))]
    pallas_call x1, Pallas kernels: 105 us -> 103 us  [per_device(): pl.pallas_call(kernel, out_shape=(jax.ShapeDtypeStruct((12, 192, 128), BF...]
where the time goes in v3:
time: 112 us
  Pallas kernels  103 us (92%)
  local copies, waits for them, and re-layouts  8.39 us (7%)
    pallas_call x1, Pallas kernels, per_device(): pl.pallas_call(kernel, out_shape=(jax.ShapeDtypeStruct((12, 192, 128), BF...  103 us
    unnamed x8, local copies, waits for them, and re-layouts  8.39 us

profile of v3, /device:TPU:1, one launch (start us, length us, event | category | flops | bytes accessed | tf_op | source)
XLA Modules:
  0.0 111.8 jit_solution(7423010134888114814)
XLA Ops:
  0.6 102.8 %shard_map.129 = (bf16[12,192,128]{2,1,0:T(8,128)(2,1)}, f32[2,576,512]{2,1,0:T(8,128)}, f32[512,1536]{1,0:T(8,128)}, f32[512,512]{1,0:T(8,128)}) custom-call(bf16[2,576,512]{2,1,0:T(8,128)(2,1)} %bitcast.5, s32[12,48]{1,0:T(8,128)} %region.1, bf16[512,1536]{1,0:T(8,128)(2,1)} %w_qkv_h.1, bf16[512,512]{1,0:T(8,128)(2,1)} %w_proj_h.1, ...), custom_call_target="tpu_custom_call" | custom-call | tf_op jit(solution)/shard_map/pallas_call | solution.py:593
  103.4 1.9 %copy.18 = bf16[2,6,192,128]{3,2,1,0:T(8,128)(2,1)} copy(bf16[2,6,192,128]{3,2,1,0:T(8,128)(2,1)} %bitcast.7) | data formatting | bytes 1179648
  105.3 0.0 copy-start
  105.4 3.5 %copy.19 = f32[2,12,48,512]{3,2,1,0:T(8,128)} copy(f32[2,12,48,512]{3,2,1,0:T(8,128)} %bitcast.4) | data formatting | bytes 4718592
  108.9 0.0 copy-done
  108.9 0.0 copy-start.1
  108.9 1.7 %copy.20 = f32[512,1536]{1,0:T(8,128)} copy(f32[512,1536]{1,0:T(8,128)S(1)} %copy-done) | data formatting | bytes 6291456
  110.6 0.3 copy-done.1
  110.9 1.0 copy.21
Async XLA Ops:
  105.3 3.5 %copy-start = (f32[512,1536]{1,0:T(8,128)S(1)}, f32[512,1536]{1,0:T(8,128)}, u32[]{:S(2)}) copy-start(f32[512,1536]{1,0:T(8,128)} %get-tuple-element.18) | copy-start | bytes 9437188
  108.9 2.0 %copy-start.1 = (f32[512,512]{1,0:T(8,128)S(1)}, f32[512,512]{1,0:T(8,128)}, u32[]{:S(2)}) copy-start(f32[512,512]{1,0:T(8,128)} %get-tuple-element.19) | copy-start | bytes 3145732

commit v4 on v3

--- a/solution.py
+++ b/solution.py
@@ -17,8 +17,9 @@
 EPS = 1e-05
 
 HALF = 288
+EDGE = 36
 PACK = 48
-EXT = HALF + PACK
+SIDE = 112
 WIN = 144
 TOK = 1152
 CELLS = 288
@@ -38,18 +39,28 @@
 
 
 def one_hots():
-    to_win = np.zeros((HALF, EXT), np.float32)
+    to_win = np.zeros((HALF, HALF), np.float32)
+    from_win = np.zeros((HALF + PACK, HALF), np.float32)
+    edge_in = np.zeros((4, 80, SIDE), np.float32)
     pack = np.zeros((PACK, HALF), np.float32)
-    for wc in range(4):
-        for lr in range(6):
+    unpack = np.zeros((3, HALF, SIDE), np.float32)
+    for lr in range(6):
+        for wc in range(4):
             for cw in range(WIN_LON):
                 u = wc * 72 + lr * WIN_LON + cw
                 col = WIN_LON * wc + WIN_LON // 2 + cw
-                to_win[u, lr * 48 + col if col < 48 else HALF + lr * 6 + col - 48] = 1.0
-    for lr in range(6):
+                if col < 48:
+                    to_win[u, lr * 48 + col] = from_win[lr * 48 + col, u] = 1.0
+                else:
+                    at = lr * 6 + col - 48
+                    from_win[HALF + at, u] = 1.0
+                    for half in range(4):
+                        edge_in[half, u - 216, half * EDGE + at if half < 3 else 12 + at] = 1.0
         for c in range(6):
             pack[lr * 6 + c, lr * 48 + c] = 1.0
-    return to_win, pack
+            for half in range(3):
+                unpack[half, lr * 48 + c, half * EDGE + lr * 6 + c] = 1.0
+    return to_win, from_win, edge_in, pack, unpack, pack.T
 
 
 def nn(a, b):
@@ -81,12 +92,12 @@
 
 
 def kernel(
-    tokens, region, w_qkv_h, w_proj_h, w_merge_h, d_merged, to_win_h, from_win_h, pack_h, unpack_h,
-    m_out, gx_out, gq_out, gp_out,
-    ext, packs, regions, wq, wp, wm, dm_raw, dm_send, dm_recv, to_win, from_win, pack, unpack,
-    xw, keyw, normed, q, k, v, block_q, block_d, staged, soft, mixed_t, normed_t, mixed, tmp, b_send, b_pack, b_lat, b_packr,
-    grid_s, g, d_in, d_str, d_ext, d_packs, d_win, d_mix, d_qkv, merged, merged_in, merged_all,
-    r_send, r_pack, r_lat, r_packr,
+    tokens, region, w_qkv_h, w_proj_h, w_merge_h, d_merged, to_win_h, from_win_h, edge_in_h, pack_h, unpack_h, corner_h,
+    m_out, gx_out, gw_out,
+    ext, side, corner, regions, wq, wp, wm, dm_raw, dm_send, dm_recv, to_win, from_win, edge_in, pack, unpack, uncorner, loose, packed,
+    xw, keyw, normed, q, k, v, block_q, block_d, staged, soft, mixed_t, normed_t, mixed, tmp, b_send, b_diag, b_lat, b_side, b_corner,
+    grid_s, g, d_in, d_str, d_ext, d_side, d_corner, d_win, d_mix, d_qkv, merged, merged_in, merged_all,
+    r_send, r_diag, r_lat, r_side, r_corner,
     grads, core_send, core_recv, send1, recv1, send2, recv2, total,
     local_sem, halo_send, halo_recv, a2a_send, a2a_recv, ar_send, ar_recv,
 ):
@@ -141,9 +152,9 @@
             rows, place = pl.ds(hb * 144, 144), pl.ds(lev * 144, 144)
             loads.append(local(len(loads), tokens.at[lev, rows], ext.at[hb, place, pl.ds(0, D)]))
     for src, dst in ((region, regions), (pack_h, pack), (to_win_h, to_win), (d_merged, dm_raw), (w_qkv_h, wq), (w_merge_h, wm),
-                     (w_proj_h, wp), (from_win_h, from_win), (unpack_h, unpack)):
+                     (w_proj_h, wp), (from_win_h, from_win), (unpack_h, unpack), (edge_in_h, edge_in), (corner_h, uncorner)):
         loads.append(local(len(loads), src, dst))
-    grid_loads, (l_reg, l_pack, l_to, l_dm, l_wq, l_wm, l_wp, l_from, l_un) = loads[:8], loads[8:]
+    grid_loads, (l_reg, l_pack, l_to, l_dm, l_wq, l_wm, l_wp, l_from, l_un, l_edge, l_corner) = loads[:8], loads[8:]
 
     barrier = pltpu.get_barrier_semaphore()
     peers = [(south, lon), (north, lon), (south, east), (north, west)]
@@ -160,39 +171,51 @@
     for copy in grid_loads:
         copy.wait()
     l_reg.wait()
-    corner = lax.broadcasted_iota(jnp.int32, (48, 48), 0) == lax.broadcasted_iota(jnp.int32, (48, 48), 1)
+    diagonal = lax.broadcasted_iota(jnp.int32, (48, 48), 0) == lax.broadcasted_iota(jnp.int32, (48, 48), 1)
     for row in range(12):
-        column = jnp.sum(jnp.where(corner, regions[row:row + 1, :].astype(F32), 0.0), 1, keepdims=True)
+        column = jnp.sum(jnp.where(diagonal, regions[row:row + 1, :].astype(F32), 0.0), 1, keepdims=True)
         if row < WIN_LAT // 2:
             column = column + jnp.where(lat == 0, 4.0, 0.0)
         for lev in range(LEV):
             at = lev * 144 + row % 3 * 48
             ext[row // 3, at:at + 48, D:] = jnp.broadcast_to(column, (48, 128)).astype(BF)
     l_pack.wait()
-    for hb in range(4):
-        packs[hb] = nn(pack[...], ext[hb, 0:HALF, :]).astype(BF)
-    pl.semaphore_wait(barrier, len(peers))
-
-    def send_halo(full, small, base):
-        out = [remote(full.at[0, pl.ds(0, HALF)], full.at[4, pl.ds(0, HALF)], halo_send, halo_recv, base, (north, lon))]
-        for hb in range(4):
-            to = (north, west) if hb == 0 else (lat, west)
-            out.append(remote(small.at[hb], full.at[hb if hb else 4, pl.ds(HALF, PACK)], halo_send, halo_recv, base + 1 + hb, to))
+    def gather_edges(number, full, width):
+        for i, hb in enumerate((1, 2, 3, 0)):
+            loose[i * EDGE:(i + 1) * EDGE, 0:width] = nn(pack[...], full[hb])[0:EDGE]
+        packed[number, :, 0:width] = loose[:, 0:width].astype(BF)
+
+    def send_halo(number, full, to_side, to_corner, width):
+        lanes = pl.ds(0, width)
+        out = [
+            remote(full.at[0], full.at[4], halo_send, halo_recv, number * 3, (north, lon)),
+            remote(packed.at[number, pl.ds(0, SIDE), lanes], to_side, halo_send, halo_recv, number * 3 + 1, (lat, west)),
+            remote(packed.at[number, pl.ds(96, PACK), lanes], to_corner, halo_send, halo_recv, number * 3 + 2, (north, west)),
+        ]
         started.extend(out)
         return out
 
-    halo = send_halo(ext, packs, 0)
+    gather_edges(0, ext, 640)
+    pl.semaphore_wait(barrier, len(peers))
+    halo = send_halo(0, ext, side, corner, 640)
 
     l_dm.wait()
     for s in range(8):
         part = dm_raw[:, s * 24:(s + 1) * 24, :].astype(F32)
         dm_send[s] = part.reshape(CELLS, 128).astype(BF)
-    def window_rows(half, first, moved, wide):
-        for i in range(moved.shape[0] // 72):
-            at = ((half // 2) * 4 + first + i) * WIN + (half % 2) * 72
-            wide[at:at + 72, :] = moved[i * 72:(i + 1) * 72, :D]
-            if moved.shape[1] > D:
-                keyw[at:at + 72, :] = moved[i * 72:(i + 1) * 72, D:]
+    def window_rows(half, first, last, full, to_side, to_corner, wide):
+        moved = nn(to_win[first * 72:last * 72, :], full[half + 1])
+        for wc in range(first, last):
+            at = ((half // 2) * 4 + wc) * WIN + (half % 2) * 72
+            part = moved[(wc - first) * 72:(wc - first + 1) * 72, :]
+            if wc == 3:
+                if half == 3:
+                    part = part + nn(edge_in[3, :, 0:PACK], to_corner[...])[0:72]
+                else:
+                    part = part + nn(edge_in[half], to_side[...])[0:72]
+            wide[at:at + 72, :] = part[:, :D]
+            if part.shape[1] > D:
+                keyw[at:at + 72, :] = part[:, D:]
 
     def norm_window(w, _):
         rows = pl.ds(pl.multiple_of(w * WIN, WIN), WIN)
@@ -267,14 +290,10 @@
 
     l_to.wait()
     for half in range(2):
-        window_rows(half, 0, nn(to_win[0:WIN, 0:HALF], ext[half + 1, 0:HALF, :]), xw)
+        window_rows(half, 0, 2, ext, side, corner, xw)
     lax.fori_loop(0, 2, norm_window, 0)
     l_wq.wait()
     project_pair(0, 0)
-    attend_pair(0, 0)
-
-    for copy in halo:
-        copy.wait_recv()
     mine = pl.ds(pl.multiple_of(lon * 128, 128), 128)
     a2a_in = []
     for by in range(1, 8):
@@ -282,10 +301,15 @@
         a2a_in.append(remote(dm_send.at[to], dm_recv.at[:, mine], a2a_send, a2a_recv, by - 1, (lat, to)))
     started.extend(a2a_in)
     dm_recv[:, mine] = dm_send[lon]
+    attend_pair(0, 0)
+
+    for copy in halo:
+        copy.wait_recv()
+    l_edge.wait()
     for half in range(2):
-        window_rows(half, 2, nn(to_win[WIN:, :], ext[half + 1]), xw)
+        window_rows(half, 2, 4, ext, side, corner, xw)
     for half in range(2, 4):
-        window_rows(half, 0, nn(to_win[...], ext[half + 1]), xw)
+        window_rows(half, 0, 4, ext, side, corner, xw)
     lax.fori_loop(2, 8, norm_window, 0)
     lax.fori_loop(1, 4, project_pair, 0)
     lax.fori_loop(2, 4, attend_pair, 0)
@@ -293,22 +317,31 @@
     l_wp.wait()
     l_from.wait()
     l_un.wait()
-
-    def to_grid(half, base, lat_send, lat_recv, pack_send, pack_recv, keep):
+    l_corner.wait()
+
+    def to_grid(half, number, lat_send, lat_recv, diag_send, to_side, to_corner, keep):
         first = (half // 2) * 4
         block = jnp.concatenate([tmp[(first + wc) * WIN + (half % 2) * 72:(first + wc) * WIN + (half % 2) * 72 + 72, :] for wc in range(4)], 0)
         moved = nn(from_win[...], block.astype(BF))
-        pack_send[half] = moved[HALF:, :].astype(BF)
         out = []
         if half == 3:
+            loose[3 * EDGE:, 0:D] = jnp.zeros((EDGE, D), F32)
+            diag_send[...] = moved[HALF:, :].astype(BF)
             lat_send[...] = moved[:HALF, :].astype(BF)
-            out.append(remote(lat_send, lat_recv, halo_send, halo_recv, base, (south, lon)))
-            out.append(remote(pack_send.at[3], pack_recv.at[0], halo_send, halo_recv, base + 1, (south, east)))
+            out.append(remote(lat_send, lat_recv, halo_send, halo_recv, number * 3, (south, lon)))
+            out.append(remote(diag_send, to_corner, halo_send, halo_recv, number * 3 + 2, (south, east)))
         else:
             put(keep, slice((half + 1) * HALF, (half + 2) * HALF), moved[:HALF, :])
-            out.append(remote(pack_send.at[half], pack_recv.at[half + 1], halo_send, halo_recv, base + 2 + half, (lat, east)))
+            loose[half * EDGE:(half + 1) * EDGE, 0:D] = moved[HALF:HALF + EDGE, :]
+        if half == 0:
+            packed[number, :, 0:D] = loose[:, 0:D].astype(BF)
+            sides = packed.at[number, pl.ds(0, SIDE), pl.ds(0, D)]
+            out.append(remote(sides, to_side, halo_send, halo_recv, number * 3 + 1, (lat, east)))
         started.extend(out)
         return out
+
+    def from_edges(hb, to_side, to_corner):
+        return nn(uncorner[...], to_corner[...]) if hb == 0 else nn(unpack[hb - 1], to_side[...])
 
     branch_halo = []
     for band in (1, 0):
@@ -317,7 +350,7 @@
         rows = slice(band * 576, (band + 1) * 576)
         tmp[rows, :] = nn(mixed[rows, :], wp[...])
         for half in (band * 2 + 1, band * 2):
-            branch_halo += to_grid(half, 5, b_send, b_lat, b_pack, b_packr, grid_s)
+            branch_halo += to_grid(half, 1, b_send, b_lat, b_diag, b_side, b_corner, grid_s)
 
     l_wm.wait()
     for copy in a2a_in:
@@ -338,7 +371,7 @@
     for hb in range(4):
         at = slice(hb * HALF, (hb + 1) * HALF)
         own = b_lat[...].astype(F32) if hb == 0 else take(grid_s, at)
-        full = own + nn(unpack[...], b_packr[hb])
+        full = own + from_edges(hb, b_side, b_corner)
         put(grid_s, at, (ext[hb, 0:HALF, 0:D].astype(F32) + full).astype(BF).astype(F32))
 
     def cell_rows(p, lev, i):
@@ -369,10 +402,9 @@
                 put(d_str, pl.ds(cell_rows(p, lev, i), 24, stride=2), d_part[at:at + 24, :])
 
     for hb in range(4):
-        d_ext[hb, 0:HALF, :] = take(d_str, slice(hb * HALF, (hb + 1) * HALF)).astype(BF)
-    for hb in range(4):
-        d_packs[hb] = nn(pack[...], d_ext[hb, 0:HALF, :]).astype(BF)
-    d_halo = send_halo(d_ext, d_packs, 10)
+        d_ext[hb] = take(d_str, slice(hb * HALF, (hb + 1) * HALF)).astype(BF)
+    gather_edges(2, d_ext, D)
+    d_halo = send_halo(2, d_ext, d_side, d_corner, D)
 
     for n in range(2):
         cols = slice(n * 512, (n + 1) * 512)
@@ -481,12 +513,11 @@
         flying = [send(37, total.at[m, rows1], total.at[m, rows1], other)]
         yield
         flying[0].wait_recv()
-        grads[m] = total[m].astype(F32)
-        outs.append(local(m, grads.at[m], gq_out.at[:, pl.ds((m - 1) * D, D)] if m else gp_out))
+        outs.append(local(m, total.at[m], gw_out.at[:, pl.ds(m * D, D)]))
         yield
 
     for half in range(2):
-        window_rows(half, 0, nn(to_win[0:WIN, 0:HALF], d_ext[half + 1, 0:HALF, :]), tmp)
+        window_rows(half, 0, 2, d_ext, d_side, d_corner, tmp)
     back_pair(0, 0)
     attend_back_pair(0, 0)
     for copy in d_halo:
@@ -497,16 +528,16 @@
     merged_out = started[-7:]
     merged_in[lon] = merged[lon]
     for half in range(2):
-        window_rows(half, 2, nn(to_win[WIN:, :], d_ext[half + 1]), tmp)
+        window_rows(half, 2, 4, d_ext, d_side, d_corner, tmp)
     for half in range(2, 4):
-        window_rows(half, 0, nn(to_win[...], d_ext[half + 1]), tmp)
+        window_rows(half, 0, 4, d_ext, d_side, d_corner, tmp)
     lax.fori_loop(1, 4, back_pair, 0)
     grads[0] = nn(mixed_t[...], d_win[...])
     sums = [summed(0)]
     next(sums[0])
     for i in (1, 2, 3):
         attend_back_pair(i, 0)
-        if i != 2:
+        if i == 1:
             next(sums[0])
 
     for m in range(3):
@@ -528,7 +559,7 @@
     for band in (1, 0):
         norm_back_band(band, 0)
         for half in (band * 2 + 1, band * 2):
-            roll_halo += to_grid(half, 15, r_send, r_lat, r_pack, r_packr, grid_s)
+            roll_halo += to_grid(half, 3, r_send, r_lat, r_diag, r_side, r_corner, grid_s)
         for step in sums:
             next(step)
 
@@ -546,7 +577,7 @@
     for hb in range(4):
         at = slice(hb * HALF, (hb + 1) * HALF)
         own = r_lat[...].astype(F32) if hb == 0 else take(grid_s, at)
-        put(d_str, at, take(d_str, at) + own + nn(unpack[...], r_packr[hb]))
+        put(d_str, at, take(d_str, at) + own + from_edges(hb, r_side, r_corner))
         for lev in range(LEV):
             for c in range(4):
                 src = d_str.at[c, pl.ds(hb * HALF + lev * 144, 144)]
@@ -564,22 +595,52 @@
         copy.wait()
 
 
+def finish(m_in, gx_in, gw_in, m_out, gx_out, gq_out, gp_out, m_v, gx_v, gw_v, wide, in_sem, out_sem):
+    ins, outs = [], []
+
+    def start(sems, held, src, dst):
+        copy = pltpu.make_async_copy(src, dst, sems.at[len(held)])
+        copy.start()
+        held.append(copy)
+
+    quarters = [pl.ds(i * 128, 128) for i in range(4)]
+    halves = [(lev, pl.ds(i * 288, 288)) for lev in range(LEV) for i in range(2)]
+    for rows in quarters:
+        start(in_sem, ins, gw_in.at[rows], gw_v.at[rows])
+    for at in halves:
+        start(in_sem, ins, gx_in.at[at], gx_v.at[at])
+    start(in_sem, ins, m_in, m_v)
+    for i, rows in enumerate(quarters):
+        ins[i].wait()
+        wide[rows, :] = gw_v[rows, :].astype(F32)
+        start(out_sem, outs, wide.at[rows, pl.ds(D, 3 * D)], gq_out.at[rows])
+        start(out_sem, outs, wide.at[rows, pl.ds(0, D)], gp_out.at[rows])
+    for i, at in enumerate(halves):
+        ins[4 + i].wait()
+        start(out_sem, outs, gx_v.at[at], gx_out.at[at])
+    ins[8].wait()
+    start(out_sem, outs, m_v, m_out)
+    for copy in outs:
+        copy.wait()
+
+
 def vmem(*shape, dtype=BF):
     return pltpu.VMEM(shape, dtype)
 
 
 SCRATCH = [
-    vmem(5, EXT, 640), vmem(4, PACK, 640), vmem(12, 48, dtype=jnp.int32), vmem(D, 3 * D), vmem(D, D), vmem(4 * D, D2),
-    vmem(12, 192, 128), vmem(8, CELLS, 128), vmem(CELLS, D2), vmem(HALF, EXT), vmem(EXT, HALF), vmem(PACK, HALF), vmem(HALF, PACK),
+    vmem(5, HALF, 640), vmem(SIDE, 640), vmem(PACK, 640), vmem(12, 48, dtype=jnp.int32), vmem(D, 3 * D), vmem(D, D), vmem(4 * D, D2),
+    vmem(12, 192, 128), vmem(8, CELLS, 128), vmem(CELLS, D2), vmem(HALF, HALF), vmem(HALF + PACK, HALF), vmem(4, 80, SIDE),
+    vmem(PACK, HALF), vmem(3, HALF, SIDE), vmem(HALF, PACK), vmem(4 * EDGE, 640, dtype=F32), vmem(4, 4 * EDGE, 640),
     vmem(TOK, D, dtype=F32), vmem(TOK, 128, dtype=F32), vmem(TOK, D), vmem(TOK, D), vmem(TOK, D), vmem(TOK, D),
     vmem(2, 1152, 256), vmem(2, 1152, 256), vmem(2, 1152, 128, dtype=F32), vmem(8, WIN, 1152, dtype=F32), vmem(D, TOK), vmem(D, TOK), vmem(TOK, D), vmem(TOK, D, dtype=F32),
-    vmem(HALF, D), vmem(4, PACK, D), vmem(HALF, D), vmem(4, PACK, D),
+    vmem(HALF, D), vmem(PACK, D), vmem(HALF, D), vmem(SIDE, D), vmem(PACK, D),
     vmem(4, TOK, 128, dtype=F32), vmem(4, CELLS, D, dtype=F32), vmem(4, CELLS, D, dtype=F32), vmem(4, TOK, 128, dtype=F32),
-    vmem(5, EXT, D), vmem(4, PACK, D), vmem(TOK, D), vmem(TOK, D), vmem(TOK, 3 * D), vmem(8, CELLS, 128), vmem(8, CELLS, 128), vmem(12, 192, 128, dtype=F32),
-    vmem(HALF, D), vmem(4, PACK, D), vmem(HALF, D), vmem(4, PACK, D),
+    vmem(5, HALF, D), vmem(SIDE, D), vmem(PACK, D), vmem(TOK, D), vmem(TOK, D), vmem(TOK, 3 * D), vmem(8, CELLS, 128), vmem(8, CELLS, 128), vmem(12, 192, 128, dtype=F32),
+    vmem(HALF, D), vmem(PACK, D), vmem(HALF, D), vmem(SIDE, D), vmem(PACK, D),
     vmem(4, D, D, dtype=F32), vmem(4, 256, D), vmem(4, 256, D), vmem(4, 256, D),
     vmem(4, 3, 64, D), vmem(4, 64, D), vmem(4, 15, 16, 128), vmem(4, D, D),
-    pltpu.SemaphoreType.DMA((38,)), pltpu.SemaphoreType.DMA((20,)), pltpu.SemaphoreType.DMA((20,)),
+    pltpu.SemaphoreType.DMA((38,)), pltpu.SemaphoreType.DMA((12,)), pltpu.SemaphoreType.DMA((12,)),
     pltpu.SemaphoreType.DMA((14,)), pltpu.SemaphoreType.DMA((14,)),
     pltpu.SemaphoreType.DMA((152,)), pltpu.SemaphoreType.DMA((152,)),
 ]
@@ -587,19 +648,17 @@
 
 def per_device(tokens, region, w_qkv, w_proj, w_merge, d_merged):
     levels, lat_rows, lon_cols, feature = tokens.shape
-    to_win, pack = one_hots()
-    consts = [jnp.asarray(a, BF) for a in (to_win, to_win.T, pack, pack.T)]
+    consts = [jnp.asarray(a, BF) for a in one_hots()]
     anywhere = pl.BlockSpec(memory_space=pl.ANY)
-    m_out, gx_out, gq_out, gp_out = pl.pallas_call(
+    m_out, gx_out, gw_out = pl.pallas_call(
         kernel,
         out_shape=(
             jax.ShapeDtypeStruct((12, 192, 128), BF),
             jax.ShapeDtypeStruct((levels, 576, feature), F32),
-            jax.ShapeDtypeStruct((D, 3 * D), F32),
-            jax.ShapeDtypeStruct((D, D), F32),
+            jax.ShapeDtypeStruct((D, 4 * D), BF),
         ),
-        in_specs=[anywhere] * 10,
-        out_specs=(anywhere,) * 4,
+        in_specs=[anywhere] * 12,
+        out_specs=(anywhere,) * 3,
         scratch_shapes=SCRATCH,
         compiler_params=pltpu.CompilerParams(
             collective_id=0, has_side_effects=True, vmem_limit_bytes=64 * 1024 * 1024
@@ -608,9 +667,25 @@
         tokens.reshape(levels, 576, feature), region, w_qkv, w_proj, w_merge,
         d_merged.reshape(12, 192, 128), *consts,
     )
-    merged = m_out.reshape(levels, 6, 192, 128)
-    grad_x = gx_out.reshape(levels, lat_rows, lon_cols, feature)
-    return (merged, grad_x, gq_out, gp_out)
+    merged, grad_x, grad_qkv, grad_proj = pl.pallas_call(
+        finish,
+        out_shape=(
+            jax.ShapeDtypeStruct((12, 192, 128), BF),
+            jax.ShapeDtypeStruct((levels, 576, feature), F32),
+            jax.ShapeDtypeStruct((D, 3 * D), F32),
+            jax.ShapeDtypeStruct((D, D), F32),
+        ),
+        in_specs=[anywhere] * 3,
+        out_specs=(anywhere,) * 4,
+        scratch_shapes=[
+            vmem(12, 192, 128), vmem(LEV, 576, D, dtype=F32), vmem(D, 4 * D), vmem(D, 4 * D, dtype=F32),
+            pltpu.SemaphoreType.DMA((9,)), pltpu.SemaphoreType.DMA((13,)),
+        ],
+        compiler_params=pltpu.CompilerParams(vmem_limit_bytes=32 * 1024 * 1024),
+    )(m_out, gx_out, gw_out)
+    return (
+        merged.reshape(levels, 6, 192, 128), grad_x.reshape(levels, lat_rows, lon_cols, feature), grad_qkv, grad_proj
+    )
 
 
 def solution(mesh):

time: 112 us -> 113 us (level)
  Pallas kernels: 103 us -> 108 us
  local copies, waits for them, and re-layouts: 8.39 us -> 4.31 us
    unnamed x8 -> x6, local copies, waits for them, and re-layouts: 8.39 us -> 4.31 us
    pallas_call x0 -> x1, Pallas kernels: none -> 3.9 us  [per_device(): pl.pallas_call(finish, out_shape=(jax.ShapeDtypeStruct((12, 192, 128), BF...]
where the time goes in v4:
time: 113 us
  Pallas kernels  108 us (96%)
  local copies, waits for them, and re-layouts  4.31 us (4%)
    pallas_call x1, Pallas kernels, per_device(): pl.pallas_call(kernel, out_shape=(jax.ShapeDtypeStruct((12, 192, 128), BF...  104 us
    unnamed x6, local copies, waits for them, and re-layouts  4.31 us
    pallas_call x1, Pallas kernels, per_device(): pl.pallas_call(finish, out_shape=(jax.ShapeDtypeStruct((12, 192, 128), BF...  3.9 us

profile of v4, /device:TPU:1, one launch (start us, length us, event | category | flops | bytes accessed | tf_op | source)
XLA Modules:
  0.0 112.8 jit_solution(1508081513709131459)
XLA Ops:
  0.6 103.7 %shard_map.147 = (bf16[12,192,128]{2,1,0:T(8,128)(2,1)}, f32[2,576,512]{2,1,0:T(8,128)}, bf16[512,2048]{1,0:T(8,128)(2,1)}) custom-call(bf16[2,576,512]{2,1,0:T(8,128)(2,1)} %bitcast.4, s32[12,48]{1,0:T(8,128)} %region.1, bf16[512,1536]{1,0:T(8,128)(2,1)} %w_qkv_h.1, bf16[512,512]{1,0:T(8,128)(2,1)} %w_proj_h.1, bf16[2048,1024]{1,0:T(8,128)(2,1)} %w_merge_h.1, ...), custom_call_target="tpu_custom_call" | custom-call | tf_op jit(solution)/shard_map/pallas_call | solution.py:653
  104.4 0.0 copy-start
  104.4 1.7 %copy-done = f32[2,576,512]{2,1,0:T(8,128)S(1)} copy-done((f32[2,576,512]{2,1,0:T(8,128)S(1)}, f32[2,576,512]{2,1,0:T(8,128)}, u32[]{:S(2)}) %copy-start) | copy-done | bytes 2359320
  106.0 0.0 copy-start.1
  106.0 1.6 %copy-done.1 = bf16[512,2048]{1,0:T(8,128)(2,1)S(1)} copy-done((bf16[512,2048]{1,0:T(8,128)(2,1)S(1)}, bf16[512,2048]{1,0:T(8,128)(2,1)}, u32[]{:S(2)}) %copy-start.1) | copy-done | bytes 2097176
  107.6 0.0 copy-start.2
  107.6 1.1 copy-done.2
  108.7 3.9 %shard_map.148 = (bf16[12,192,128]{2,1,0:T(8,128)(2,1)}, f32[2,576,512]{2,1,0:T(8,128)}, f32[512,1536]{1,0:T(8,128)}, f32[512,512]{1,0:T(8,128)}) custom-call(bf16[12,192,128]{2,1,0:T(8,128)(2,1)S(1)} %copy-done.2, f32[2,576,512]{2,1,0:T(8,128)S(1)} %copy-done, bf16[512,2048]{1,0:T(8,128)(2,1)S(1)} %copy-done.1), custom_call_target="tpu_custom_call" | custom-call | tf_op jit(solution)/shard_map/pallas_call | solution.py:670
Async XLA Ops:
  104.4 1.7 %copy-start = (f32[2,576,512]{2,1,0:T(8,128)S(1)}, f32[2,576,512]{2,1,0:T(8,128)}, u32[]{:S(2)}) copy-start(f32[2,576,512]{2,1,0:T(8,128)} %get-tuple-element.12.gx_in) | copy-start | bytes 7077892
  106.0 1.6 %copy-start.1 = (bf16[512,2048]{1,0:T(8,128)(2,1)S(1)}, bf16[512,2048]{1,0:T(8,128)(2,1)}, u32[]{:S(2)}) copy-start(bf16[512,2048]{1,0:T(8,128)(2,1)} %get-tuple-element.13.gw_in) | copy-start | bytes 6291460
  107.6 1.1 copy-start.2

commit v5 on v4

--- a/solution.py
+++ b/solution.py
@@ -296,15 +296,21 @@
     project_pair(0, 0)
     mine = pl.ds(pl.multiple_of(lon * 128, 128), 128)
     a2a_in = []
-    for by in range(1, 8):
-        to = lax.rem(lon + by, 8)
-        a2a_in.append(remote(dm_send.at[to], dm_recv.at[:, mine], a2a_send, a2a_recv, by - 1, (lat, to)))
-    started.extend(a2a_in)
+
+    def send_cotangents(steps):
+        for by in steps:
+            to = lax.rem(lon + by, 8)
+            copy = remote(dm_send.at[to], dm_recv.at[:, mine], a2a_send, a2a_recv, by - 1, (lat, to))
+            a2a_in.append(copy)
+            started.append(copy)
+
+    send_cotangents((2, 4, 6))
     dm_recv[:, mine] = dm_send[lon]
     attend_pair(0, 0)
 
     for copy in halo:
         copy.wait_recv()
+    send_cotangents((1, 3, 5, 7))
     l_edge.wait()
     for half in range(2):
         window_rows(half, 2, 4, ext, side, corner, xw)
@@ -328,15 +334,19 @@
             loose[3 * EDGE:, 0:D] = jnp.zeros((EDGE, D), F32)
             diag_send[...] = moved[HALF:, :].astype(BF)
             lat_send[...] = moved[:HALF, :].astype(BF)
-            out.append(remote(lat_send, lat_recv, halo_send, halo_recv, number * 3, (south, lon)))
-            out.append(remote(diag_send, to_corner, halo_send, halo_recv, number * 3 + 2, (south, east)))
+            out.append((lat_send, lat_recv, number * 3, (south, lon)))
+            out.append((diag_send, to_corner, number * 3 + 2, (south, east)))
         else:
             put(keep, slice((half + 1) * HALF, (half + 2) * HALF), moved[:HALF, :])
             loose[half * EDGE:(half + 1) * EDGE, 0:D] = moved[HALF:HALF + EDGE, :]
         if half == 0:
             packed[number, :, 0:D] = loose[:, 0:D].astype(BF)
             sides = packed.at[number, pl.ds(0, SIDE), pl.ds(0, D)]
-            out.append(remote(sides, to_side, halo_send, halo_recv, number * 3 + 1, (lat, east)))
+            out.append((sides, to_side, number * 3 + 1, (lat, east)))
+        return out
+
+    def launch(parts):
+        out = [remote(src, dst, halo_send, halo_recv, i, to) for src, dst, i, to in parts]
         started.extend(out)
         return out
 
@@ -350,7 +360,7 @@
         rows = slice(band * 576, (band + 1) * 576)
         tmp[rows, :] = nn(mixed[rows, :], wp[...])
         for half in (band * 2 + 1, band * 2):
-            branch_halo += to_grid(half, 1, b_send, b_lat, b_diag, b_side, b_corner, grid_s)
+            branch_halo += launch(to_grid(half, 1, b_send, b_lat, b_diag, b_side, b_corner, grid_s))
 
     l_wm.wait()
     for copy in a2a_in:
@@ -555,13 +565,17 @@
         )
         return 0
 
-    roll_halo = []
+    roll_parts = []
     for band in (1, 0):
         norm_back_band(band, 0)
+        if band == 1:
+            for step in sums:
+                next(step)
         for half in (band * 2 + 1, band * 2):
-            roll_halo += to_grid(half, 3, r_send, r_lat, r_diag, r_side, r_corner, grid_s)
-        for step in sums:
-            next(step)
+            roll_parts += to_grid(half, 3, r_send, r_lat, r_diag, r_side, r_corner, grid_s)
+    for step in sums:
+        next(step)
+    roll_halo = launch(roll_parts)
 
     for copy in merged_out:
         copy.wait_recv()
@@ -569,8 +583,9 @@
         merged_all[:, s * 24:(s + 1) * 24, :] = merged_in[s].astype(F32).reshape(12, 24, 128)
     dm_raw[...] = merged_all[...].astype(BF)
     outs.append(local(4, dm_raw, m_out))
-    for step in sums:
-        next(step)
+    for _ in range(2):
+        for step in sums:
+            next(step)
 
     for copy in roll_halo:
         copy.wait_recv()
@@ -583,8 +598,6 @@
                 src = d_str.at[c, pl.ds(hb * HALF + lev * 144, 144)]
                 to = gx_out.at[lev, pl.ds(hb * 144, 144), pl.ds(c * 128, 128)]
                 outs.append(local(5 + hb * 8 + lev * 4 + c, src, to))
-        for step in sums:
-            next(step, None)
     for _ in range(8):
         for step in sums:
             next(step, None)
@@ -681,7 +694,7 @@
             vmem(12, 192, 128), vmem(LEV, 576, D, dtype=F32), vmem(D, 4 * D), vmem(D, 4 * D, dtype=F32),
             pltpu.SemaphoreType.DMA((9,)), pltpu.SemaphoreType.DMA((13,)),
         ],
-        compiler_params=pltpu.CompilerParams(vmem_limit_bytes=32 * 1024 * 1024),
+        compiler_params=pltpu.CompilerParams(vmem_limit_bytes=64 * 1024 * 1024),
     )(m_out, gx_out, gw_out)
     return (
         merged.reshape(levels, 6, 192, 128), grad_x.reshape(levels, lat_rows, lon_cols, feature), grad_qkv, grad_proj

time: 113 us -> 102 us (0.903)
  Pallas kernels: 108 us -> 101 us
  local copies, waits for them, and re-layouts: 4.31 us -> 0 us
    pallas_call x1, Pallas kernels: 104 us -> 96.9 us  [per_device(): pl.pallas_call(kernel, out_shape=(jax.ShapeDtypeStruct((12, 192, 128), BF...]
    unnamed x6 -> x0, local copies, waits for them, and re-layouts: 4.31 us -> none
where the time goes in v5:
time: 102 us
  Pallas kernels  101 us (99%)
    pallas_call x1, Pallas kernels, per_device(): pl.pallas_call(kernel, out_shape=(jax.ShapeDtypeStruct((12, 192, 128), BF...  96.9 us
    pallas_call x1, Pallas kernels, per_device(): pl.pallas_call(finish, out_shape=(jax.ShapeDtypeStruct((12, 192, 128), BF...  4.39 us

profile of v5, /device:TPU:1, one launch (start us, length us, event | category | flops | bytes accessed | tf_op | source)
XLA Modules:
  0.0 102.2 jit_solution(6954410430876120301)
XLA Ops:
  0.6 96.9 %shard_map.147 = (bf16[12,192,128]{2,1,0:T(8,128)(2,1)}, f32[2,576,512]{2,1,0:T(8,128)}, bf16[512,2048]{1,0:T(8,128)(2,1)}) custom-call(bf16[2,576,512]{2,1,0:T(8,128)(2,1)} %bitcast.4, s32[12,48]{1,0:T(8,128)} %region.1, bf16[512,1536]{1,0:T(8,128)(2,1)} %w_qkv_h.1, bf16[512,512]{1,0:T(8,128)(2,1)} %w_proj_h.1, bf16[2048,1024]{1,0:T(8,128)(2,1)} %w_merge_h.1, ...), custom_call_target="tpu_custom_call" | custom-call | tf_op jit(solution)/shard_map/pallas_call | solution.py:666
  97.6 4.4 %shard_map.148 = (bf16[12,192,128]{2,1,0:T(8,128)(2,1)}, f32[2,576,512]{2,1,0:T(8,128)}, f32[512,1536]{1,0:T(8,128)}, f32[512,512]{1,0:T(8,128)}) custom-call(bf16[12,192,128]{2,1,0:T(8,128)(2,1)} %get-tuple-element.11.m_in, f32[2,576,512]{2,1,0:T(8,128)} %get-tuple-element.12.gx_in, bf16[512,2048]{1,0:T(8,128)(2,1)} %get-tuple-element.13.gw_in), custom_call_target="tpu_custom_call" | custom-call | tf_op jit(solution)/shard_map/pallas_call | solution.py:683

commit v6 on v5

--- a/solution.py
+++ b/solution.py
@@ -94,7 +94,7 @@
 def kernel(
     tokens, region, w_qkv_h, w_proj_h, w_merge_h, d_merged, to_win_h, from_win_h, edge_in_h, pack_h, unpack_h, corner_h,
     m_out, gx_out, gw_out,
-    ext, side, corner, regions, wq, wp, wm, dm_raw, dm_send, dm_recv, to_win, from_win, edge_in, pack, unpack, uncorner, loose, packed,
+    ext, side, corner, regions, region_s, region_e, region_se, keys, key_side, key_corner, key_loose, wq, wp, wm, dm_raw, dm_send, dm_recv, to_win, from_win, edge_in, pack, unpack, uncorner, loose, packed,
     xw, keyw, normed, q, k, v, block_q, block_d, staged, soft, mixed_t, normed_t, mixed, tmp, b_send, b_diag, b_lat, b_side, b_corner,
     grid_s, g, d_in, d_str, d_ext, d_side, d_corner, d_win, d_mix, d_qkv, merged, merged_in, merged_all,
     r_send, r_diag, r_lat, r_side, r_corner,
@@ -150,7 +150,7 @@
     for hb in range(4):
         for lev in range(LEV):
             rows, place = pl.ds(hb * 144, 144), pl.ds(lev * 144, 144)
-            loads.append(local(len(loads), tokens.at[lev, rows], ext.at[hb, place, pl.ds(0, D)]))
+            loads.append(local(len(loads), tokens.at[lev, rows], ext.at[hb, place]))
     for src, dst in ((region, regions), (pack_h, pack), (to_win_h, to_win), (d_merged, dm_raw), (w_qkv_h, wq), (w_merge_h, wm),
                      (w_proj_h, wp), (from_win_h, from_win), (unpack_h, unpack), (edge_in_h, edge_in), (corner_h, uncorner)):
         loads.append(local(len(loads), src, dst))
@@ -171,51 +171,54 @@
     for copy in grid_loads:
         copy.wait()
     l_reg.wait()
-    diagonal = lax.broadcasted_iota(jnp.int32, (48, 48), 0) == lax.broadcasted_iota(jnp.int32, (48, 48), 1)
-    for row in range(12):
-        column = jnp.sum(jnp.where(diagonal, regions[row:row + 1, :].astype(F32), 0.0), 1, keepdims=True)
-        if row < WIN_LAT // 2:
-            column = column + jnp.where(lat == 0, 4.0, 0.0)
-        for lev in range(LEV):
-            at = lev * 144 + row % 3 * 48
-            ext[row // 3, at:at + 48, D:] = jnp.broadcast_to(column, (48, 128)).astype(BF)
     l_pack.wait()
-    def gather_edges(number, full, width):
+
+    def gather_edges(number, full):
         for i, hb in enumerate((1, 2, 3, 0)):
-            loose[i * EDGE:(i + 1) * EDGE, 0:width] = nn(pack[...], full[hb])[0:EDGE]
-        packed[number, :, 0:width] = loose[:, 0:width].astype(BF)
-
-    def send_halo(number, full, to_side, to_corner, width):
-        lanes = pl.ds(0, width)
+            loose[i * EDGE:(i + 1) * EDGE, :] = nn(pack[...], full[hb])[0:EDGE]
+        packed[number] = loose[...].astype(BF)
+
+    def send_halo(number, full, to_side, to_corner):
         out = [
             remote(full.at[0], full.at[4], halo_send, halo_recv, number * 3, (north, lon)),
-            remote(packed.at[number, pl.ds(0, SIDE), lanes], to_side, halo_send, halo_recv, number * 3 + 1, (lat, west)),
-            remote(packed.at[number, pl.ds(96, PACK), lanes], to_corner, halo_send, halo_recv, number * 3 + 2, (north, west)),
+            remote(packed.at[number, pl.ds(0, SIDE)], to_side, halo_send, halo_recv, number * 3 + 1, (lat, west)),
+            remote(packed.at[number, pl.ds(96, PACK)], to_corner, halo_send, halo_recv, number * 3 + 2, (north, west)),
         ]
         started.extend(out)
         return out
 
-    gather_edges(0, ext, 640)
+    gather_edges(0, ext)
     pl.semaphore_wait(barrier, len(peers))
-    halo = send_halo(0, ext, side, corner, 640)
+    halo = send_halo(0, ext, side, corner)
+    for i, (there, to) in enumerate(((region_s, (north, lon)), (region_e, (lat, west)), (region_se, (north, west)))):
+        halo.append(remote(regions, there, halo_send, halo_recv, 12 + i, to))
+    started.extend(halo[3:])
 
     l_dm.wait()
     for s in range(8):
         part = dm_raw[:, s * 24:(s + 1) * 24, :].astype(F32)
         dm_send[s] = part.reshape(CELLS, 128).astype(BF)
     def window_rows(half, first, last, full, to_side, to_corner, wide):
-        moved = nn(to_win[first * 72:last * 72, :], full[half + 1])
+        low_row, high_row = first * 72 // 16 * 16, -(-last * 72 // 16) * 16
+        moved = nn(to_win[low_row:high_row, :], full[half + 1])
         for wc in range(first, last):
             at = ((half // 2) * 4 + wc) * WIN + (half % 2) * 72
-            part = moved[(wc - first) * 72:(wc - first + 1) * 72, :]
+            part = moved[wc * 72 - low_row:(wc + 1) * 72 - low_row, :]
             if wc == 3:
                 if half == 3:
                     part = part + nn(edge_in[3, :, 0:PACK], to_corner[...])[0:72]
                 else:
                     part = part + nn(edge_in[half], to_side[...])[0:72]
-            wide[at:at + 72, :] = part[:, :D]
-            if part.shape[1] > D:
-                keyw[at:at + 72, :] = part[:, D:]
+            wide[at:at + 72, :] = part
+
+    diagonal = lax.broadcasted_iota(jnp.int32, (48, 48), 0) == lax.broadcasted_iota(jnp.int32, (48, 48), 1)
+
+    def key_rows(source, first, extra):
+        rows = []
+        for row in range(first, first + 3):
+            column = jnp.sum(jnp.where(diagonal, source[row:row + 1, :].astype(F32), 0.0), 1, keepdims=True)
+            rows.append(jnp.broadcast_to(column + extra, (48, 128)))
+        return jnp.concatenate(rows * LEV, 0).astype(BF)
 
     def norm_window(w, _):
         rows = pl.ds(pl.multiple_of(w * WIN, WIN), WIN)
@@ -223,12 +226,17 @@
         normed[rows, :] = (centred * inverse).astype(BF)
         return 0
 
-    def project_pair(i, _):
-        rows = pl.ds(pl.multiple_of(i * 288, 288), 288)
+    def project(rows):
         block = normed[rows, :]
         q[rows, :] = (nn(block, wq[:, 0:D]).astype(BF) * 0.125).astype(BF)
         k[rows, :] = nn(block, wq[:, D:2 * D]).astype(BF)
         v[rows, :] = nn(block, wq[:, 2 * D:3 * D]).astype(BF)
+
+    def later_rows(i):
+        return pl.ds(pl.multiple_of(3 * WIN + i * 240, 16), 240)
+
+    def project_later(i, _):
+        project(later_rows(i))
         return 0
 
     lane = lax.broadcasted_iota(jnp.int32, (WIN, 128), 1)
@@ -290,10 +298,14 @@
 
     l_to.wait()
     for half in range(2):
-        window_rows(half, 0, 2, ext, side, corner, xw)
-    lax.fori_loop(0, 2, norm_window, 0)
+        window_rows(half, 0, 3, ext, side, corner, xw)
+    lax.fori_loop(0, 3, norm_window, 0)
+    for half in range(3):
+        keys[half + 1] = key_rows(regions, 3 * half + 3, 0.0)
+    for half in range(2):
+        window_rows(half, 0, 3, keys, key_side, key_corner, keyw)
     l_wq.wait()
-    project_pair(0, 0)
+    project(slice(0, 3 * WIN))
     mine = pl.ds(pl.multiple_of(lon * 128, 128), 128)
     a2a_in = []
 
@@ -307,17 +319,25 @@
     send_cotangents((2, 4, 6))
     dm_recv[:, mine] = dm_send[lon]
     attend_pair(0, 0)
+    attend(2, block_q.at[0], staged.at[0])
 
     for copy in halo:
         copy.wait_recv()
     send_cotangents((1, 3, 5, 7))
     l_edge.wait()
-    for half in range(2):
-        window_rows(half, 2, 4, ext, side, corner, xw)
-    for half in range(2, 4):
-        window_rows(half, 0, 4, ext, side, corner, xw)
-    lax.fori_loop(2, 8, norm_window, 0)
-    lax.fori_loop(1, 4, project_pair, 0)
+    edge_key = jnp.where(lat == 15, 4.0, 0.0)
+    keys[4] = key_rows(region_s, 0, edge_key)
+    for half in range(4):
+        near = key_rows(region_e, 3 * half + 3, 0.0) if half < 3 else key_rows(region_se, 0, edge_key)
+        key_loose[half * EDGE:(half + 1) * EDGE, :] = nn(pack[...], near)[0:EDGE]
+    key_side[...] = key_loose[0:SIDE, :].astype(BF)
+    key_corner[...] = key_loose[96:, :].astype(BF)
+    for half in range(4):
+        first = 3 if half < 2 else 0
+        window_rows(half, first, 4, ext, side, corner, xw)
+        window_rows(half, first, 4, keys, key_side, key_corner, keyw)
+    lax.fori_loop(3, 8, norm_window, 0)
+    lax.fori_loop(0, 3, project_later, 0)
     lax.fori_loop(2, 4, attend_pair, 0)
 
     l_wp.wait()
@@ -331,17 +351,17 @@
         moved = nn(from_win[...], block.astype(BF))
         out = []
         if half == 3:
-            loose[3 * EDGE:, 0:D] = jnp.zeros((EDGE, D), F32)
+            loose[3 * EDGE:, :] = jnp.zeros((EDGE, D), F32)
             diag_send[...] = moved[HALF:, :].astype(BF)
             lat_send[...] = moved[:HALF, :].astype(BF)
             out.append((lat_send, lat_recv, number * 3, (south, lon)))
             out.append((diag_send, to_corner, number * 3 + 2, (south, east)))
         else:
             put(keep, slice((half + 1) * HALF, (half + 2) * HALF), moved[:HALF, :])
-            loose[half * EDGE:(half + 1) * EDGE, 0:D] = moved[HALF:HALF + EDGE, :]
+            loose[half * EDGE:(half + 1) * EDGE, :] = moved[HALF:HALF + EDGE, :]
         if half == 0:
-            packed[number, :, 0:D] = loose[:, 0:D].astype(BF)
-            sides = packed.at[number, pl.ds(0, SIDE), pl.ds(0, D)]
+            packed[number] = loose[...].astype(BF)
+            sides = packed.at[number, pl.ds(0, SIDE)]
             out.append((sides, to_side, number * 3 + 1, (lat, east)))
         return out
 
@@ -356,7 +376,7 @@
     branch_halo = []
     for band in (1, 0):
         if band == 0:
-            attend_pair(1, 0)
+            attend(3, block_q.at[0], staged.at[0])
         rows = slice(band * 576, (band + 1) * 576)
         tmp[rows, :] = nn(mixed[rows, :], wp[...])
         for half in (band * 2 + 1, band * 2):
@@ -382,7 +402,7 @@
         at = slice(hb * HALF, (hb + 1) * HALF)
         own = b_lat[...].astype(F32) if hb == 0 else take(grid_s, at)
         full = own + from_edges(hb, b_side, b_corner)
-        put(grid_s, at, (ext[hb, 0:HALF, 0:D].astype(F32) + full).astype(BF).astype(F32))
+        put(grid_s, at, (ext[hb].astype(F32) + full).astype(BF).astype(F32))
 
     def cell_rows(p, lev, i):
         row = 2 * i + p % 2
@@ -413,8 +433,8 @@
 
     for hb in range(4):
         d_ext[hb] = take(d_str, slice(hb * HALF, (hb + 1) * HALF)).astype(BF)
-    gather_edges(2, d_ext, D)
-    d_halo = send_halo(2, d_ext, d_side, d_corner, D)
+    gather_edges(2, d_ext)
+    d_halo = send_halo(2, d_ext, d_side, d_corner)
 
     for n in range(2):
         cols = slice(n * 512, (n + 1) * 512)
@@ -423,11 +443,13 @@
             sums = sums + nn(g[p].astype(BF), wm[p * D:(p + 1) * D, cols])
         for s in range(4):
             merged[n * 4 + s] = sums[:, s * 128:(s + 1) * 128].astype(BF)
-    def back_pair(i, _):
-        rows = pl.ds(pl.multiple_of(i * 288, 288), 288)
+    def back(rows):
         block = tmp[rows, :].astype(BF)
         d_win[rows, :] = block
         d_mix[rows, :] = nt(block, wp[...]).astype(BF)
+
+    def back_later(i, _):
+        back(later_rows(i))
         return 0
 
     def attend_back(w, q_b, d_b, stage):
@@ -527,9 +549,10 @@
         yield
 
     for half in range(2):
-        window_rows(half, 0, 2, d_ext, d_side, d_corner, tmp)
-    back_pair(0, 0)
+        window_rows(half, 0, 3, d_ext, d_side, d_corner, tmp)
+    back(slice(0, 3 * WIN))
     attend_back_pair(0, 0)
+    attend_back(2, block_q.at[0], block_d.at[0], staged.at[0])
     for copy in d_halo:
         copy.wait_recv()
     for by in range(1, 8):
@@ -537,18 +560,16 @@
         started.append(remote(merged.at[to], merged_in.at[lon], a2a_send, a2a_recv, 6 + by, (lat, to)))
     merged_out = started[-7:]
     merged_in[lon] = merged[lon]
-    for half in range(2):
-        window_rows(half, 2, 4, d_ext, d_side, d_corner, tmp)
-    for half in range(2, 4):
-        window_rows(half, 0, 4, d_ext, d_side, d_corner, tmp)
-    lax.fori_loop(1, 4, back_pair, 0)
+    for half in range(4):
+        window_rows(half, 3 if half < 2 else 0, 4, d_ext, d_side, d_corner, tmp)
+    lax.fori_loop(0, 3, back_later, 0)
     grads[0] = nn(mixed_t[...], d_win[...])
     sums = [summed(0)]
     next(sums[0])
-    for i in (1, 2, 3):
-        attend_back_pair(i, 0)
-        if i == 1:
-            next(sums[0])
+    attend_back_pair(2, 0)
+    next(sums[0])
+    attend_back_pair(3, 0)
+    attend_back(3, block_q.at[0], block_d.at[0], staged.at[0])
 
     for m in range(3):
         grads[m + 1] = nn(normed_t[...], d_qkv[:, m * D:(m + 1) * D])
@@ -642,9 +663,10 @@
 
 
 SCRATCH = [
-    vmem(5, HALF, 640), vmem(SIDE, 640), vmem(PACK, 640), vmem(12, 48, dtype=jnp.int32), vmem(D, 3 * D), vmem(D, D), vmem(4 * D, D2),
+    vmem(5, HALF, D), vmem(SIDE, D), vmem(PACK, D)] + [vmem(12, 48, dtype=jnp.int32)] * 4 + [
+    vmem(5, HALF, 128), vmem(SIDE, 128), vmem(PACK, 128), vmem(4 * EDGE, 128, dtype=F32), vmem(D, 3 * D), vmem(D, D), vmem(4 * D, D2),
     vmem(12, 192, 128), vmem(8, CELLS, 128), vmem(CELLS, D2), vmem(HALF, HALF), vmem(HALF + PACK, HALF), vmem(4, 80, SIDE),
-    vmem(PACK, HALF), vmem(3, HALF, SIDE), vmem(HALF, PACK), vmem(4 * EDGE, 640, dtype=F32), vmem(4, 4 * EDGE, 640),
+    vmem(PACK, HALF), vmem(3, HALF, SIDE), vmem(HALF, PACK), vmem(4 * EDGE, D, dtype=F32), vmem(4, 4 * EDGE, D),
     vmem(TOK, D, dtype=F32), vmem(TOK, 128, dtype=F32), vmem(TOK, D), vmem(TOK, D), vmem(TOK, D), vmem(TOK, D),
     vmem(2, 1152, 256), vmem(2, 1152, 256), vmem(2, 1152, 128, dtype=F32), vmem(8, WIN, 1152, dtype=F32), vmem(D, TOK), vmem(D, TOK), vmem(TOK, D), vmem(TOK, D, dtype=F32),
     vmem(HALF, D), vmem(PACK, D), vmem(HALF, D), vmem(SIDE, D), vmem(PACK, D),
@@ -653,7 +675,7 @@
     vmem(HALF, D), vmem(PACK, D), vmem(HALF, D), vmem(SIDE, D), vmem(PACK, D),
     vmem(4, D, D, dtype=F32), vmem(4, 256, D), vmem(4, 256, D), vmem(4, 256, D),
     vmem(4, 3, 64, D), vmem(4, 64, D), vmem(4, 15, 16, 128), vmem(4, D, D),
-    pltpu.SemaphoreType.DMA((38,)), pltpu.SemaphoreType.DMA((12,)), pltpu.SemaphoreType.DMA((12,)),
+    pltpu.SemaphoreType.DMA((38,)), pltpu.SemaphoreType.DMA((15,)), pltpu.SemaphoreType.DMA((15,)),
     pltpu.SemaphoreType.DMA((14,)), pltpu.SemaphoreType.DMA((14,)),
     pltpu.SemaphoreType.DMA((152,)), pltpu.SemaphoreType.DMA((152,)),
 ]

time: 102 us -> 98.5 us (0.966)
  Pallas kernels: 101 us -> 97.5 us
    pallas_call x1, Pallas kernels: 96.9 us -> 93.1 us  [per_device(): pl.pallas_call(kernel, out_shape=(jax.ShapeDtypeStruct((12, 192, 128), BF...]
where the time goes in v6:
time: 98.5 us; the launch traced here: 98.3 us
  Pallas kernels  97.5 us (99%)
    pallas_call x1, Pallas kernels, per_device(): pl.pallas_call(kernel, out_shape=(jax.ShapeDtypeStruct((12, 192, 128), BF...  93.1 us
    pallas_call x1, Pallas kernels, per_device(): pl.pallas_call(finish, out_shape=(jax.ShapeDtypeStruct((12, 192, 128), BF...  4.39 us

profile of v6, /device:TPU:1, one launch (start us, length us, event | category | flops | bytes accessed | tf_op | source)
XLA Modules:
  0.0 98.3 jit_solution(1641350065820299115)
XLA Ops:
  0.6 93.1 %shard_map.147 = (bf16[12,192,128]{2,1,0:T(8,128)(2,1)}, f32[2,576,512]{2,1,0:T(8,128)}, bf16[512,2048]{1,0:T(8,128)(2,1)}) custom-call(bf16[2,576,512]{2,1,0:T(8,128)(2,1)} %bitcast.4, s32[12,48]{1,0:T(8,128)} %region.1, bf16[512,1536]{1,0:T(8,128)(2,1)} %w_qkv_h.1, bf16[512,512]{1,0:T(8,128)(2,1)} %w_proj_h.1, bf16[2048,1024]{1,0:T(8,128)(2,1)} %w_merge_h.1, ...), custom_call_target="tpu_custom_call" | custom-call | tf_op jit(solution)/shard_map/pallas_call | solution.py:688
  93.8 4.4 %shard_map.148 = (bf16[12,192,128]{2,1,0:T(8,128)(2,1)}, f32[2,576,512]{2,1,0:T(8,128)}, f32[512,1536]{1,0:T(8,128)}, f32[512,512]{1,0:T(8,128)}) custom-call(bf16[12,192,128]{2,1,0:T(8,128)(2,1)} %get-tuple-element.11.m_in, f32[2,576,512]{2,1,0:T(8,128)} %get-tuple-element.12.gx_in, bf16[512,2048]{1,0:T(8,128)(2,1)} %get-tuple-element.13.gw_in), custom_call_target="tpu_custom_call" | custom-call | tf_op jit(solution)/shard_map/pallas_call | solution.py:705

commit v7 on v6

--- a/solution.py
+++ b/solution.py
@@ -97,7 +97,7 @@
     ext, side, corner, regions, region_s, region_e, region_se, keys, key_side, key_corner, key_loose, wq, wp, wm, dm_raw, dm_send, dm_recv, to_win, from_win, edge_in, pack, unpack, uncorner, loose, packed,
     xw, keyw, normed, q, k, v, block_q, block_d, staged, soft, mixed_t, normed_t, mixed, tmp, b_send, b_diag, b_lat, b_side, b_corner,
     grid_s, g, d_in, d_str, d_ext, d_side, d_corner, d_win, d_mix, d_qkv, merged, merged_in, merged_all,
-    r_send, r_diag, r_lat, r_side, r_corner,
+    r_send, r_diag, r_lat, r_side, r_corner, gx_all,
     grads, core_send, core_recv, send1, recv1, send2, recv2, total,
     local_sem, halo_send, halo_recv, a2a_send, a2a_recv, ar_send, ar_recv,
 ):
@@ -151,10 +151,8 @@
         for lev in range(LEV):
             rows, place = pl.ds(hb * 144, 144), pl.ds(lev * 144, 144)
             loads.append(local(len(loads), tokens.at[lev, rows], ext.at[hb, place]))
-    for src, dst in ((region, regions), (pack_h, pack), (to_win_h, to_win), (d_merged, dm_raw), (w_qkv_h, wq), (w_merge_h, wm),
-                     (w_proj_h, wp), (from_win_h, from_win), (unpack_h, unpack), (edge_in_h, edge_in), (corner_h, uncorner)):
-        loads.append(local(len(loads), src, dst))
-    grid_loads, (l_reg, l_pack, l_to, l_dm, l_wq, l_wm, l_wp, l_from, l_un, l_edge, l_corner) = loads[:8], loads[8:]
+    l_reg = local(8, region, regions)
+    l_pack = local(9, pack_h, pack)
 
     barrier = pltpu.get_barrier_semaphore()
     peers = [(south, lon), (north, lon), (south, east), (north, west)]
@@ -168,8 +166,13 @@
     for peer in peers:
         pl.semaphore_signal(barrier, inc=1, device_id=peer, device_id_type=MESH)
 
-    for copy in grid_loads:
+    for copy in loads:
         copy.wait()
+    later = ((to_win_h, to_win), (w_qkv_h, wq), (d_merged, dm_raw), (edge_in_h, edge_in), (w_proj_h, wp),
+             (from_win_h, from_win), (unpack_h, unpack), (corner_h, uncorner), (w_merge_h, wm))
+    l_to, l_wq, l_dm, l_edge, l_wp, l_from, l_un, l_corner, l_wm = [
+        local(10 + i, src, dst) for i, (src, dst) in enumerate(later)
+    ]
     l_reg.wait()
     l_pack.wait()
 
@@ -443,6 +446,18 @@
             sums = sums + nn(g[p].astype(BF), wm[p * D:(p + 1) * D, cols])
         for s in range(4):
             merged[n * 4 + s] = sums[:, s * 128:(s + 1) * 128].astype(BF)
+    merged_out = []
+
+    def send_merged(steps):
+        for by in steps:
+            to = lax.rem(lon + by, 8)
+            copy = remote(merged.at[to], merged_in.at[lon], a2a_send, a2a_recv, 6 + by, (lat, to))
+            merged_out.append(copy)
+            started.append(copy)
+
+    send_merged((2, 4, 6))
+    merged_in[lon] = merged[lon]
+
     def back(rows):
         block = tmp[rows, :].astype(BF)
         d_win[rows, :] = block
@@ -555,11 +570,7 @@
     attend_back(2, block_q.at[0], block_d.at[0], staged.at[0])
     for copy in d_halo:
         copy.wait_recv()
-    for by in range(1, 8):
-        to = lax.rem(lon + by, 8)
-        started.append(remote(merged.at[to], merged_in.at[lon], a2a_send, a2a_recv, 6 + by, (lat, to)))
-    merged_out = started[-7:]
-    merged_in[lon] = merged[lon]
+    send_merged((1, 3, 5, 7))
     for half in range(4):
         window_rows(half, 3 if half < 2 else 0, 4, d_ext, d_side, d_corner, tmp)
     lax.fori_loop(0, 3, back_later, 0)
@@ -613,12 +624,10 @@
     for hb in range(4):
         at = slice(hb * HALF, (hb + 1) * HALF)
         own = r_lat[...].astype(F32) if hb == 0 else take(grid_s, at)
-        put(d_str, at, take(d_str, at) + own + from_edges(hb, r_side, r_corner))
+        gx_all[hb] = (take(d_str, at) + own + from_edges(hb, r_side, r_corner)).astype(BF)
         for lev in range(LEV):
-            for c in range(4):
-                src = d_str.at[c, pl.ds(hb * HALF + lev * 144, 144)]
-                to = gx_out.at[lev, pl.ds(hb * 144, 144), pl.ds(c * 128, 128)]
-                outs.append(local(5 + hb * 8 + lev * 4 + c, src, to))
+            src = gx_all.at[hb, pl.ds(lev * 144, 144)]
+            outs.append(local(5 + hb * 2 + lev, src, gx_out.at[lev, pl.ds(hb * 144, 144)]))
     for _ in range(8):
         for step in sums:
             next(step, None)
@@ -629,7 +638,7 @@
         copy.wait()
 
 
-def finish(m_in, gx_in, gw_in, m_out, gx_out, gq_out, gp_out, m_v, gx_v, gw_v, wide, in_sem, out_sem):
+def finish(m_in, gx_in, gw_in, m_out, gx_out, gq_out, gp_out, m_v, gx_v, gx_wide, gw_v, wide, in_sem, out_sem):
     ins, outs = [], []
 
     def start(sems, held, src, dst):
@@ -651,7 +660,8 @@
         start(out_sem, outs, wide.at[rows, pl.ds(0, D)], gp_out.at[rows])
     for i, at in enumerate(halves):
         ins[4 + i].wait()
-        start(out_sem, outs, gx_v.at[at], gx_out.at[at])
+        gx_wide[at] = gx_v[at].astype(F32)
+        start(out_sem, outs, gx_wide.at[at], gx_out.at[at])
     ins[8].wait()
     start(out_sem, outs, m_v, m_out)
     for copy in outs:
@@ -672,7 +682,7 @@
     vmem(HALF, D), vmem(PACK, D), vmem(HALF, D), vmem(SIDE, D), vmem(PACK, D),
     vmem(4, TOK, 128, dtype=F32), vmem(4, CELLS, D, dtype=F32), vmem(4, CELLS, D, dtype=F32), vmem(4, TOK, 128, dtype=F32),
     vmem(5, HALF, D), vmem(SIDE, D), vmem(PACK, D), vmem(TOK, D), vmem(TOK, D), vmem(TOK, 3 * D), vmem(8, CELLS, 128), vmem(8, CELLS, 128), vmem(12, 192, 128, dtype=F32),
-    vmem(HALF, D), vmem(PACK, D), vmem(HALF, D), vmem(SIDE, D), vmem(PACK, D),
+    vmem(HALF, D), vmem(PACK, D), vmem(HALF, D), vmem(SIDE, D), vmem(PACK, D), vmem(4, HALF, D),
     vmem(4, D, D, dtype=F32), vmem(4, 256, D), vmem(4, 256, D), vmem(4, 256, D),
     vmem(4, 3, 64, D), vmem(4, 64, D), vmem(4, 15, 16, 128), vmem(4, D, D),
     pltpu.SemaphoreType.DMA((38,)), pltpu.SemaphoreType.DMA((15,)), pltpu.SemaphoreType.DMA((15,)),
@@ -689,7 +699,7 @@
         kernel,
         out_shape=(
             jax.ShapeDtypeStruct((12, 192, 128), BF),
-            jax.ShapeDtypeStruct((levels, 576, feature), F32),
+            jax.ShapeDtypeStruct((levels, 576, feature), BF),
             jax.ShapeDtypeStruct((D, 4 * D), BF),
         ),
         in_specs=[anywhere] * 12,
@@ -713,7 +723,7 @@
         in_specs=[anywhere] * 3,
         out_specs=(anywhere,) * 4,
         scratch_shapes=[
-            vmem(12, 192, 128), vmem(LEV, 576, D, dtype=F32), vmem(D, 4 * D), vmem(D, 4 * D, dtype=F32),
+            vmem(12, 192, 128), vmem(LEV, 576, D), vmem(LEV, 576, D, dtype=F32), vmem(D, 4 * D), vmem(D, 4 * D, dtype=F32),
             pltpu.SemaphoreType.DMA((9,)), pltpu.SemaphoreType.DMA((13,)),
         ],
         compiler_params=pltpu.CompilerParams(vmem_limit_bytes=64 * 1024 * 1024),

time: 98.5 us -> 98.7 us (level)
  no operation moved by 1% of the time
where the time goes in v7:
time: 98.7 us; the launch traced here: 98.5 us
  Pallas kernels  97.7 us (99%)
    pallas_call x1, Pallas kernels, per_device(): pl.pallas_call(kernel, out_shape=(jax.ShapeDtypeStruct((12, 192, 128), BF...  93.5 us
    pallas_call x1, Pallas kernels, per_device(): pl.pallas_call(finish, out_shape=(jax.ShapeDtypeStruct((12, 192, 128), BF...  4.21 us

profile of v7, /device:TPU:1, one launch (start us, length us, event | category | flops | bytes accessed | tf_op | source)
XLA Modules:
  0.0 98.5 jit_solution(3097678511120663113)
XLA Ops:
  0.6 93.5 %shard_map.147 = (bf16[12,192,128]{2,1,0:T(8,128)(2,1)}, bf16[2,576,512]{2,1,0:T(8,128)(2,1)}, bf16[512,2048]{1,0:T(8,128)(2,1)}) custom-call(bf16[2,576,512]{2,1,0:T(8,128)(2,1)} %bitcast.4, s32[12,48]{1,0:T(8,128)} %region.1, bf16[512,1536]{1,0:T(8,128)(2,1)} %w_qkv_h.1, bf16[512,512]{1,0:T(8,128)(2,1)} %w_proj_h.1, bf16[2048,1024]{1,0:T(8,128)(2,1)} %w_merge_h.1, ...), custom_call_target="tpu_custom_call" | custom-call | tf_op jit(solution)/shard_map/pallas_call | solution.py:698
  94.1 4.2 %shard_map.148 = (bf16[12,192,128]{2,1,0:T(8,128)(2,1)}, f32[2,576,512]{2,1,0:T(8,128)}, f32[512,1536]{1,0:T(8,128)}, f32[512,512]{1,0:T(8,128)}) custom-call(bf16[12,192,128]{2,1,0:T(8,128)(2,1)} %get-tuple-element.11.m_in, bf16[2,576,512]{2,1,0:T(8,128)(2,1)} %get-tuple-element.12.gx_in, bf16[512,2048]{1,0:T(8,128)(2,1)} %get-tuple-element.13.gw_in), custom_call_target="tpu_custom_call" | custom-call | tf_op jit(solution)/shard_map/pallas_call | solution.py:715

commit v8 on v7

--- a/solution.py
+++ b/solution.py
@@ -508,7 +508,7 @@
         (move1, at1), (_, at2), (_, at3) = [along[axis] for axis in orders[m]]
 
         def send(i, src, dst, to):
-            copy = remote(src, dst, ar_send, ar_recv, m * 38 + i, to)
+            copy = remote(src, dst, ar_send, ar_recv, m * 41 + i, to)
             started.append(copy)
             return copy
 
@@ -542,7 +542,7 @@
         row1 = core * 256
         row2 = row1 + at1 * 64
         row3 = row2 + at2 * 16
-        rows1, rows2, rows3 = [pl.ds(pl.multiple_of(r, n), n) for r, n in ((row1, 256), (row2, 64), (row3, 16))]
+        rows2, rows3 = [pl.ds(pl.multiple_of(r, n), n) for r, n in ((row2, 64), (row3, 16))]
         cols = pl.ds(pl.multiple_of(at3 * 128, 128), 128)
         own = acc1[m, pl.ds(pl.multiple_of(at2 * 16, 16), 16), cols]
         for j in range(15):
@@ -554,12 +554,15 @@
         for copy in flying:
             copy.wait_recv()
         flying = [send(33 + by, total.at[m, rows2], total.at[m, rows2], move1(by)) for by in range(1, 4)]
+        crossing = [send(37, total.at[m, rows2], total.at[m, rows2], other)]
         yield
-        for copy in flying:
+        for by, copy in enumerate(flying, 1):
             copy.wait_recv()
-        flying = [send(37, total.at[m, rows1], total.at[m, rows1], other)]
+            rows = pl.ds(pl.multiple_of(row1 + lax.rem(at1 + 4 - by, 4) * 64, 64), 64)
+            crossing.append(send(37 + by, total.at[m, rows], total.at[m, rows], other))
         yield
-        flying[0].wait_recv()
+        for copy in crossing:
+            copy.wait_recv()
         outs.append(local(m, total.at[m], gw_out.at[:, pl.ds(m * D, D)]))
         yield
 
@@ -582,10 +585,12 @@
     attend_back_pair(3, 0)
     attend_back(3, block_q.at[0], block_d.at[0], staged.at[0])
 
+    proj_sum = sums.pop()
     for m in range(3):
         grads[m + 1] = nn(normed_t[...], d_qkv[:, m * D:(m + 1) * D])
         sums.append(summed(m + 1))
-        next(sums[m + 1])
+        next(sums[m])
+    sums.append(proj_sum)
 
     def norm_back_band(band, _):
         rows = pl.ds(pl.multiple_of(band * 576, 576), 576)
@@ -687,7 +692,7 @@
     vmem(4, 3, 64, D), vmem(4, 64, D), vmem(4, 15, 16, 128), vmem(4, D, D),
     pltpu.SemaphoreType.DMA((38,)), pltpu.SemaphoreType.DMA((15,)), pltpu.SemaphoreType.DMA((15,)),
     pltpu.SemaphoreType.DMA((14,)), pltpu.SemaphoreType.DMA((14,)),
-    pltpu.SemaphoreType.DMA((152,)), pltpu.SemaphoreType.DMA((152,)),
+    pltpu.SemaphoreType.DMA((164,)), pltpu.SemaphoreType.DMA((164,)),
 ]
 
 

time: 98.7 us -> 100 us (1.013)
  Pallas kernels: 97.7 us -> 99.1 us
    pallas_call x1, Pallas kernels: 93.5 us -> 94.9 us  [per_device(): pl.pallas_call(kernel, out_shape=(jax.ShapeDtypeStruct((12, 192, 128), BF...]
where the time goes in v8:
time: 100 us; the launch traced here: 99.9 us
  Pallas kernels  99.1 us (99%)
    pallas_call x1, Pallas kernels, per_device(): pl.pallas_call(kernel, out_shape=(jax.ShapeDtypeStruct((12, 192, 128), BF...  94.9 us
    pallas_call x1, Pallas kernels, per_device(): pl.pallas_call(finish, out_shape=(jax.ShapeDtypeStruct((12, 192, 128), BF...  4.21 us

profile of v8, /device:TPU:1, one launch (start us, length us, event | category | flops | bytes accessed | tf_op | source)
XLA Modules:
  0.0 99.9 jit_solution(18284646245265182845)
XLA Ops:
  0.6 94.9 %shard_map.147 = (bf16[12,192,128]{2,1,0:T(8,128)(2,1)}, bf16[2,576,512]{2,1,0:T(8,128)(2,1)}, bf16[512,2048]{1,0:T(8,128)(2,1)}) custom-call(bf16[2,576,512]{2,1,0:T(8,128)(2,1)} %bitcast.4, s32[12,48]{1,0:T(8,128)} %region.1, bf16[512,1536]{1,0:T(8,128)(2,1)} %w_qkv_h.1, bf16[512,512]{1,0:T(8,128)(2,1)} %w_proj_h.1, bf16[2048,1024]{1,0:T(8,128)(2,1)} %w_merge_h.1, ...), custom_call_target="tpu_custom_call" | custom-call | tf_op jit(solution)/shard_map/pallas_call | solution.py:703
  95.5 4.2 %shard_map.148 = (bf16[12,192,128]{2,1,0:T(8,128)(2,1)}, f32[2,576,512]{2,1,0:T(8,128)}, f32[512,1536]{1,0:T(8,128)}, f32[512,512]{1,0:T(8,128)}) custom-call(bf16[12,192,128]{2,1,0:T(8,128)(2,1)} %get-tuple-element.11.m_in, bf16[2,576,512]{2,1,0:T(8,128)(2,1)} %get-tuple-element.12.gx_in, bf16[512,2048]{1,0:T(8,128)(2,1)} %get-tuple-element.13.gw_in), custom_call_target="tpu_custom_call" | custom-call | tf_op jit(solution)/shard_map/pallas_call | solution.py:720
